TPU v7x, 128 devices: a whole 4x4x4 slice. The times are simulated.
128 devices in a mesh: ctx: 16 (over y, x), head: 8 (over z, core).
Axes of the slice: x: 4, y: 4, z: 4, core: 2. Of those that a mesh axis runs over, the one named last changes fastest.
Arguments:
- q_nope: bfloat16 [8, 128, 128], P(None, 'head'), may hold values from -6 to 6
- q_rope: bfloat16 [8, 128, 64], P(None, 'head'), may hold values from -10 to 10
- latent_cache: bfloat16 [8, 131072, 576], P(None, 'ctx'), may hold values from -8 to 8
- lengths: int32 [8], replicated, may hold values from 16384 to 131072, as said below
- w_key_absorb: bfloat16 [128, 128, 512], P('head'), may hold values from -0.5 to 0.5
- w_value_up: bfloat16 [128, 512, 128], P('head'), may hold values from -0.25 to 0.25
- w_output: bfloat16 [16384, 7168], P('head', 'ctx'), may hold values from -0.046875 to 0.046875
- w_gate: bfloat16 [16, 7168, 2048], P('ctx', None, 'head'), may hold values from -0.0625 to 0.0625
- w_up: bfloat16 [16, 7168, 2048], P('ctx', None, 'head'), may hold values from -0.0625 to 0.0625
- w_down: bfloat16 [16, 2048, 7168], P('ctx', 'head'), may hold values from -0.125 to 0.125
- expert_ids: int32 [8, 8], replicated, may hold values from 0 to 15, all different within a row
- gate_weights: float32 [8, 8], replicated, may hold values from 0.05 to 0.4
Outputs:
- attn_out: bfloat16 [8, 7168], P(None, 'ctx')
- expert_out: bfloat16 [8, 7168], P(None, ('ctx', 'head'))
Inputs may be any that keep to these rules, and one draw needn't show every extreme that they name: `lengths`: every row has at least 16384 valid positions and row 0 has all of them.
All inputs are finite; a program needn't handle non-finite values.
Results may differ from a plain program's by a relative error of at most 0.03.
Values may be sent and summed in bfloat16 or wider, within the bound.
A program may use at most 192 MiB of HBM per device.

v0:
```python
import jax
import jax.numpy as jnp
from jax import lax
from jax.sharding import PartitionSpec as P

NOPE = 128
ROPE = 64
LAT = 512


def merged(part, axis, combine):
    gathered = jax.tree.map(lambda a: lax.all_gather(a, axis), part)

    def take(source):
        return jax.tree.map(lambda a: lax.dynamic_index_in_dim(a, source, 0, False), gathered)

    return lax.fori_loop(
        1, lax.axis_size(axis), lambda source, state: combine(state, take(source)), take(0)
    )


def join_partials(first, second):
    peak = jnp.maximum(first[0], second[0])
    left = jnp.exp(first[0] - peak)
    right = jnp.exp(second[0] - peak)
    total = first[1] * left + second[1] * right
    summed = first[2] * left[..., None] + second[2] * right[..., None]
    return (peak, total, summed)


def attend(query, cache, row_lengths, offset):
    scale = (NOPE + ROPE) ** (-0.5)
    span = cache.shape[1]
    positions = offset + jnp.arange(span, dtype=jnp.int32)
    score = jnp.einsum("bhc,btc->bht", query, cache, preferred_element_type=jnp.float32) * scale
    valid = positions[None, None, :] < row_lengths[:, None, None]
    peak = jnp.max(jnp.where(valid, score, -1e30), axis=-1)
    weight = jnp.where(valid, jnp.exp(score - peak[..., None]), 0.0)
    total = jnp.sum(weight, axis=-1)
    summed = jnp.einsum(
        "bht,btl->bhl",
        weight.astype(jnp.bfloat16),
        cache[:, :, :LAT],
        preferred_element_type=jnp.float32,
    )
    return (peak, total, summed)


def combine_slices(peak, total, summed):
    peak, total, summed = merged((peak, total, summed), "ctx", join_partials)
    return (summed / total[..., None]).astype(jnp.bfloat16)


def body(
    q_nope,
    q_rope,
    latent_cache,
    lengths,
    w_key_absorb,
    w_value_up,
    w_output,
    w_gate,
    w_up,
    w_down,
    expert_ids,
    gate_weights,
):
    rows = q_nope.shape[0]
    q_latent = jnp.einsum(
        "bhn,hnl->bhl", q_nope, w_key_absorb, preferred_element_type=jnp.float32
    ).astype(jnp.bfloat16)
    query = jnp.concatenate([q_latent, q_rope], axis=-1)
    offset = lax.axis_index("ctx") * latent_cache.shape[1]
    peak, total, summed = attend(query, latent_cache, lengths, offset)
    o_latent = combine_slices(peak, total, summed)
    head_out = jnp.einsum(
        "bhl,hln->bhn", o_latent, w_value_up, preferred_element_type=jnp.float32
    ).astype(jnp.bfloat16)
    head_out = head_out.reshape(rows, -1)
    partial_proj = jnp.dot(head_out, w_output, preferred_element_type=jnp.float32)
    attn_out = lax.psum(partial_proj, "head").astype(jnp.bfloat16)
    features = lax.all_gather(attn_out, "ctx", axis=1, tiled=True)
    wide = features.astype(jnp.float32)
    normed = (wide / jnp.sqrt(jnp.mean(wide * wide, axis=-1, keepdims=True) + 1e-06)).astype(
        jnp.bfloat16
    )
    mine = lax.axis_index("ctx")
    select = jnp.sum(gate_weights * (expert_ids == mine).astype(jnp.float32), axis=1)
    gate = jnp.dot(normed, w_gate[0], preferred_element_type=jnp.float32)
    upper = jnp.dot(normed, w_up[0], preferred_element_type=jnp.float32)
    hidden = (jax.nn.silu(gate) * upper).astype(jnp.bfloat16)
    result = jnp.dot(hidden, w_down[0], preferred_element_type=jnp.float32) * select[:, None]
    expert_out = lax.psum_scatter(result, ("ctx", "head"), scatter_dimension=1, tiled=True).astype(
        jnp.bfloat16
    )
    return (attn_out, expert_out)


def solution(mesh):
    return jax.shard_map(
        body,
        mesh=mesh,
        in_specs=(
            P(None, "head", None),
            P(None, "head", None),
            P(None, "ctx", None),
            P(),
            P("head", None, None),
            P("head", None, None),
            P("head", "ctx"),
            P("ctx", None, "head"),
            P("ctx", None, "head"),
            P("ctx", "head", None),
            P(),
            P(),
        ),
        out_specs=(P(None, "ctx"), P(None, ("ctx", "head"))),
        check_vma=False,
    )
```

profile of v0, /device:TPU:1, one launch (start us, length us, event | category | flops | bytes accessed | tf_op | source)
XLA Modules:
  0.0 271.2 jit_solution(7608450080655570873)
XLA Ops:
  7.2 0.0 copy-start
  7.2 0.0 all-gather.6.cloned.1.call-start
  7.2 0.9 copy.20
  8.2 0.8 broadcast_compare_fusion
  8.9 0.0 copy-done
  8.9 1.1 fusion.16
  10.1 28.7 %select_reduce_fusion = (f32[8,16]{1,0:T(8,128)S(1)}, f32[8,16,8192]{2,1,0:T(8,128)}) fusion(pred[8,8192]{1,0:T(8,128)(4,1)S(1)} %broadcast_compare_fusion, bf16[8,8192,576]{1,2,0:T(8,128)(2,1)} %param.16, bf16[8,16,576]{2,0,1:T(8,128)(2,1)S(1)} %pad_maximum_fusion), kind=kOutput, calls=%fused_computation.13 | convolution fusion | flops 1211105152 | bytes 79905280 | tf_op jit(solution)/shard_map/bhc,btc->bht/dot_general | solution.py:35
  38.8 27.1 %fusion.3 = f32[8,16,512]{2,1,0:T(8,128)} fusion(bf16[8,8192,576]{1,2,0:T(8,128)(2,1)} %param.16, f32[8,16,8192]{2,1,0:T(8,128)} %get-tuple-element.200, f32[8,16]{1,0:T(8,128)S(1)} %get-tuple-element.199, pred[8,8192]{1,0:T(8,128)(4,1)S(1)} %broadcast_compare_fusion), kind=kOutput, calls=%fused_computation.8 | convolution fusion | flops 1076887552 | bytes 71631360 | tf_op jit(solution)/shard_map/bht,btl->bhl/dot_general | solution.py:40
  65.9 0.0 copy-start.2
  65.9 0.0 copy-start.3
  65.9 0.0 all-gather.6.cloned.1.call-update
  66.0 19.7 %all-gather = f32[128,16]{1,0:T(8,128)S(1)} all-gather(f32[8,16]{1,0:T(8,128)S(1)} %get-tuple-element.199), channel_id=2, replica_groups=mesh['ctx'=16,'head'=8] {'ctx'}, dimensions={0}, use_global_device_ids=true | all-gather | bytes 8704 | tf_op jit(solution)/shard_map/all_gather | solution.py:12
  85.7 3.3 %fusion.11 = f32[8,16]{1,0:T(8,128)S(1)} fusion(f32[8,16,8192]{2,1,0:T(8,128)} %get-tuple-element.200, f32[8,16]{1,0:T(8,128)S(1)} %get-tuple-element.199, pred[8,8192]{1,0:T(8,128)(4,1)S(1)} %broadcast_compare_fusion), kind=kLoop, calls=%fused_computation.20 | loop fusion | flops 3145600 | bytes 4260864 | tf_op jit(solution)/shard_map/reduce_sum | solution.py:39
  89.0 18.5 %all-gather.1 = f32[128,16]{1,0:T(8,128)S(1)} all-gather(f32[8,16]{1,0:T(8,128)S(1)} %fusion.11), channel_id=3, replica_groups=mesh['ctx'=16,'head'=8] {'ctx'}, dimensions={0}, use_global_device_ids=true | all-gather | bytes 8704 | tf_op jit(solution)/shard_map/all_gather | solution.py:12
  107.5 0.0 copy-done.2
  107.5 0.0 copy-done.3
  107.5 0.1 select_reduce_fusion.1
  107.6 13.5 %all-gather.6.cloned.1.call-done = f32[128,16,512]{2,1,0:T(8,128)} async-done(((f32[8,16,512]{2,1,0:T(8,128)}), f32[128,16,512]{2,1,0:T(8,128)}) %all-gather.6.cloned.1.call-update) | async-done | bytes 4194320 | tf_op jit(solution)/shard_map/all_gather | solution.py:12
  121.2 1.0 slice.12
  122.1 16.8 %while.19 = (s32[]{:T(128)}, f32[8,16]{1,0:T(8,128)S(1)}, f32[8,16]{1,0:T(8,128)S(1)}, f32[8,16,512]{2,1,0:T(8,128)S(1)}, f32[16,8,16]{2,1,0:T(8,128)S(1)}, /*in...) while((s32[]{:T(128)}, f32[8,16]{1,0:T(8,128)S(1)}, ...), condition=%wide.region_3.4_spmd, body=%wide.region_2.3_spmd.sunk | while | flops 197381 | bytes 791703 | solution.py:17
  122.2 1.1 fusion.47
  123.3 1.1 fusion.47
  124.4 1.1 fusion.47
  125.5 1.1 fusion.47
  126.7 1.1 fusion.47
  127.8 1.1 fusion.47
  128.9 1.1 fusion.47
  130.0 1.1 fusion.47
  131.1 1.1 fusion.47
  132.3 1.1 fusion.47
  133.4 1.1 fusion.47
  134.5 1.1 fusion.47
  135.6 1.1 fusion.47
  136.7 1.1 fusion.47
  137.9 1.1 fusion.47
  139.0 0.1 divide_convert_fusion
  139.1 3.0 %fusion.26 = f32[8,448]{1,0:T(8,128)S(1)} fusion(bf16[2048,448]{0,1:T(8,128)(2,1)} %param.20, bf16[16,512,128]{2,1,0:T(8,128)(2,1)} %param.19, bf16[8,16,512]{2,1,0:T(8,128)(2,1)S(1)} %divide_convert_fusion), kind=kOutput, calls=%fused_computation.30 | convolution fusion | flops 31473664 | bytes 4077568 | tf_op jit(solution)/shard_map/dot_general | solution.py:80
  142.1 22.9 %psum.7 = bf16[8,448]{1,0:T(8,128)(2,1)S(1)} all-reduce(f32[8,448]{1,0:T(8,128)S(1)} %fusion.26), channel_id=1, replica_groups=mesh['ctx'=16,'head'=8] {'head'}, use_global_device_ids=true, to_apply=%region_4.5 | all-reduce | flops 3584 | bytes 21504 | tf_op jit(solution)/shard_map/psum | solution.py:81
  165.0 0.0 copy-start.1
  165.0 18.3 %all-gather.3 = bf16[16,448,8]{1,2,0:T(8,128)(2,1)S(1)} all-gather(bf16[1,448,8]{1,2,0:T(8,128)(2,1)S(1)} %bitcast.59), channel_id=1, replica_groups=mesh['ctx'=16,'head'=8] {'ctx'}, dimensions={0}, use_global_device_ids=true | all-gather | bytes 121856 | tf_op jit(solution)/shard_map/all_gather | solution.py:82
  183.4 0.1 reshape.65
  183.5 0.2 multiply_reduce_fusion
  183.7 2.7 fusion.8
  186.3 5.3 %convolution_multiply_fusion.1 = f32[8,7168]{1,0:T(8,128)S(1)} fusion(bf16[1,256,7168]{2,1,0:T(8,128)(2,1)} %param.23, bf16[1,7168,256]{2,1,0:T(8,128)(2,1)} %param.22, f32[8]{0:T(128)S(1)} %select_reduce_fusion.1, f32[8,256]{1,0:T(8,128)S(1)} %fusion.8, f32[7168,8]{0,1:T(8,128)S(1)} %reshape.65, f32[8]{0:T(128)S(1)} %add_sqrt_fusion), kind=kOutput, calls=%fused_computation.11 | convolution fusion | flops 58904576 | bytes 7807040 | tf_op jit(solution)/shard_map/dot_general | solution.py:92
  191.6 0.0 copy-done.1
  191.6 72.1 %all-reduce.2 = bf16[8,7168]{1,0:T(8,128)(2,1)S(1)} all-reduce(f32[8,7168]{1,0:T(8,128)S(1)} %convolution_multiply_fusion.1), channel_id=5, replica_groups=mesh['ctx'=16,'head'=8] {'ctx','head'}, use_global_device_ids=true, to_apply=%region_7.8.clone | all-reduce | flops 57344 | bytes 344064
  263.7 0.7 dynamic-slice_convert_fusion
  (21 shorter events, 0.3 us)
Async XLA Ops:
  7.2 1.8 copy-start
  7.2 114.0 %all-gather.6.cloned.1.call-start = ((), (), s32[]{:S(2)}) async-start(), calls=%async_computation | async-start | bytes 4456448 | tf_op jit(solution)/shard_map/all_gather | solution.py:12
  65.9 41.6 %copy-start.2 = (f32[8,8]{1,0:T(8,128)S(1)}, f32[8,8]{1,0:T(8,128)}, u32[]{:S(2)}) copy-start(f32[8,8]{1,0:T(8,128)} %param.25) | copy-start | bytes 772
  65.9 41.6 %copy-start.3 = (s32[8,8]{1,0:T(8,128)S(1)}, s32[8,8]{1,0:T(8,128)}, u32[]{:S(2)}) copy-start(s32[8,8]{1,0:T(8,128)} %param.24) | copy-start | bytes 772
  165.0 26.6 %copy-start.1 = (bf16[8,448]{1,0:T(8,128)(2,1)}, bf16[8,448]{1,0:T(8,128)(2,1)S(1)}, u32[]{:S(2)}) copy-start(bf16[8,448]{1,0:T(8,128)(2,1)S(1)} %psum.7) | copy-start | bytes 21508
Sparse Core Ops, SparseCore 0:
  66.1 55.0 all-gather.5
where the time goes:
time: 272 us; the launch traced here: 271 us
  blocking collectives  152 us (56%)
  matrix products  67.9 us (25%)
  other arithmetic  20.8 us (8%)
  between operations  14.1 us (5%)
  waiting for transfers between devices  13.5 us (5%)
  local copies, waits for them, and re-layouts  2.74 us (1%)
    unnamed x1, blocking collectives  72.1 us
    all_gather x2, blocking collectives, merged(): gathered = jax.tree.map(lambda a: lax.all_gather(a, axis), part)  38.2 us
    dot_general x1, matrix products, attend(): jnp.einsum('bhc,btc->bht', query, cache, preferred_element_type=jnp.float32)  28.7 us
    dot_general x1, matrix products, attend(): jnp.einsum('bht,btl->bhl', weight.astype(jnp.bfloat16), cache[:, :, :LAT]...  27.1 us
    psum x1, blocking collectives, body(): attn_out = lax.psum(partial_proj, 'head').astype(jnp.bfloat16)  22.9 us
    all_gather x1, blocking collectives, body(): features = lax.all_gather(attn_out, 'ctx', axis=1, tiled=True)  18.3 us
    add x15, other arithmetic, join_partials(): summed = first[2] * left[..., None] + second[2] * right[..., None]  16.1 us
    all_gather x1, waiting for transfers between devices, merged(): gathered = jax.tree.map(lambda a: lax.all_gather(a, axis), part)  13.5 us
  transfers between devices with their start and end apart: 1, of which 1 were waited for; matrix products, arithmetic and copies ran while one was open for 1% of the time, Pallas kernels for 0%

commit v1 on v0

v1 whole, which is shorter than its diff:
```python
import functools
import math

import jax
import jax.numpy as jnp
from jax import lax
from jax.experimental import pallas as pl
from jax.experimental.pallas import tpu as pltpu
from jax.sharding import PartitionSpec as P

ROWS = 8
HEADS = 128
NOPE = 128
ROPE = 64
LAT = 512
KEY = LAT + ROPE
D = 7168
CTX = 16
HEAD = 8
GROUP = HEADS // HEAD
SPAN = 8192 // HEAD
COLS = D // CTX
OUT = COLS // HEAD
CHUNK = 2
CHUNKS = ROWS // CHUNK
TILES = CHUNK * 4 + 1
SCALE = (NOPE + ROPE) ** -0.5 * math.log2(math.e)
MESH = pl.DeviceIdType.MESH
F32 = jnp.float32
BF16 = jnp.bfloat16


def remote(src, dst, send_sem, recv_sem, device):
    return pltpu.make_async_remote_copy(
        src_ref=src,
        dst_ref=dst,
        send_sem=send_sem,
        recv_sem=recv_sem,
        device_id=device,
        device_id_type=MESH,
    )


def loop(low, high, step):
    def run(index, carry):
        step(index)
        return carry

    lax.fori_loop(low, high, run, 0)


def pack(wide):
    wide = wide.astype(BF16).astype(F32)
    first = jnp.concatenate([wide[:, 0:128], wide[:, 128:256]], axis=0).astype(BF16)
    second = jnp.concatenate([wide[:, 256:384], wide[:, 384:512]], axis=0).astype(BF16)
    return first, second


def unpack(first, second):
    first = first.astype(F32)
    second = second.astype(F32)
    return jnp.concatenate([first[0:8], first[8:16], second[0:8], second[8:16]], axis=1)


def split_three(value):
    high = value.astype(BF16).astype(F32)
    rest = value - high
    middle = rest.astype(BF16).astype(F32)
    return high, middle, rest - middle


def lanes(shape):
    return lax.broadcasted_iota(jnp.int32, shape, len(shape) - 1)


def put_levels(levels, rows):
    lane = lanes((rows, 128))
    tile = jnp.zeros((rows, 128), F32)
    for index, level in enumerate(levels):
        for part, value in enumerate(split_three(level)):
            tile = jnp.where(lane == 3 * index + part, value, tile)
    return tile


def get_level(tile, index):
    lane = lanes(tile.shape)
    wanted = (lane >= 3 * index) & (lane < 3 * index + 3)
    return jnp.sum(jnp.where(wanted, tile, 0.0), axis=1, keepdims=True)


def weights_of(levels):
    peak = functools.reduce(jnp.maximum, levels)
    parts = [jnp.exp2(level - peak) for level in levels]
    total = functools.reduce(jnp.add, parts)
    scale = 1.0 / total
    return [part * scale for part in parts], peak + jnp.log2(total)


def kernel(
    lengths_ref,
    q_nope_ref,
    q_rope_ref,
    ids_ref,
    gates_ref,
    cache_hbm,
    absorb_hbm,
    value_hbm,
    output_hbm,
    gate_hbm,
    up_hbm,
    down_hbm,
    attn_ref,
    expert_ref,
    keys,
    absorb,
    value_up,
    w_out,
    w_gate,
    w_up,
    w_down,
    query,
    s1,
    r1,
    s2,
    r2,
    whole,
    whole_level,
    s3,
    r3,
    s4,
    r4,
    s5,
    r5,
    s6,
    r6,
    s7,
    r7,
    s8,
    r8,
    key_sem,
    weight_sem,
    q_send,
    q_from_z,
    q_from_mate,
    s1_sem,
    r1_sem,
    s2_sem,
    r2_sem,
    s3_sem,
    r3_sem,
    s4_sem,
    r4_sem,
    s5_sem,
    r5_sem,
    s6_sem,
    r6_sem,
    s7_sem,
    r7_sem,
    s8_sem,
    r8_sem,
):
    ctx = lax.axis_index("ctx")
    head = lax.axis_index("head")
    level_z = head // 2
    core = lax.rem(head, 2)
    mate = level_z * 2 + 1 - core

    def other_z(step):
        return lax.rem(level_z + step, 4)

    def other_ctx(step):
        return lax.rem(ctx + step, CTX)

    def other_head(step):
        return lax.rem(head + step, HEAD)

    absorb_copy = pltpu.make_async_copy(absorb_hbm, absorb, weight_sem.at[0])
    absorb_copy.start()
    start = pl.multiple_of(head * SPAN, SPAN)

    def key_copy(row):
        return pltpu.make_async_copy(
            cache_hbm.at[row, :, pl.ds(start, SPAN)], keys.at[row], key_sem.at[row]
        )

    loop(0, ROWS, lambda row: key_copy(row).start())
    value_copy = pltpu.make_async_copy(value_hbm.at[ctx], value_up, weight_sem.at[1])
    output_copy = pltpu.make_async_copy(output_hbm, w_out.at[pl.ds(0, COLS)], weight_sem.at[2])
    gate_copy = pltpu.make_async_copy(gate_hbm.at[0], w_gate, weight_sem.at[3])
    up_copy = pltpu.make_async_copy(up_hbm.at[0], w_up, weight_sem.at[4])
    down_copy = pltpu.make_async_copy(down_hbm.at[0], w_down, weight_sem.at[5])
    for copy in (value_copy, output_copy, gate_copy, up_copy, down_copy):
        copy.start()

    barrier = pltpu.get_barrier_semaphore()

    def greet_head(step):
        pl.semaphore_signal(
            barrier, inc=1, device_id={"head": other_head(step)}, device_id_type=MESH
        )

    def greet_ctx(step):
        pl.semaphore_signal(
            barrier, inc=1, device_id={"ctx": other_ctx(step)}, device_id_type=MESH
        )

    loop(1, HEAD, greet_head)
    loop(1, CTX, greet_ctx)

    w_out[pl.ds(COLS, 512 - COLS), :] = jnp.zeros((512 - COLS, GROUP * NOPE), BF16)
    flat = q_nope_ref[...].reshape(ROWS * GROUP, NOPE).astype(F32)
    which = lax.rem(lax.broadcasted_iota(jnp.int32, (ROWS * GROUP, NOPE), 0), GROUP)
    blocks = [jnp.where(which == h, flat, 0.0).astype(BF16) for h in range(GROUP)]
    wide_query = jnp.concatenate(blocks, axis=1)
    absorb_copy.wait()
    latent = jnp.dot(
        wide_query,
        absorb[...].reshape(GROUP * NOPE, LAT),
        preferred_element_type=F32,
    ).astype(BF16)
    mine = pl.ds(pl.multiple_of(head * GROUP, GROUP), GROUP)
    query[:, mine, 0:LAT] = latent.reshape(ROWS, GROUP, LAT)
    query[:, mine, LAT:KEY] = q_rope_ref[...]
    pl.semaphore_wait(barrier, HEAD - 1 + CTX - 1)

    def query_block(chunk, source):
        rows = pl.ds(chunk * CHUNK, CHUNK)
        return query.at[rows, pl.ds(pl.multiple_of(source * GROUP, GROUP), GROUP)]

    def query_to_z(chunk, step):
        block = query_block(chunk, head)
        z = other_z(step)
        return remote(
            block, block, q_send.at[chunk, step], q_from_z.at[chunk, level_z], {"head": z * 2 + core}
        )

    def query_from_z(chunk, step):
        z = other_z(step)
        block = query_block(chunk, z * 2 + core)
        return remote(
            block, block, q_send.at[chunk, step], q_from_z.at[chunk, z], {"head": z * 2 + core}
        )

    def query_to_mate(chunk, step):
        z = other_z(step)
        block = query_block(chunk, z * 2 + core)
        return remote(
            block, block, q_send.at[chunk, 4 + step], q_from_mate.at[chunk, z], {"head": mate}
        )

    def query_from_mate(chunk, step):
        z = other_z(step)
        block = query_block(chunk, z * 2 + 1 - core)
        return remote(
            block, block, q_send.at[chunk, 4 + step], q_from_mate.at[chunk, z], {"head": mate}
        )

    def send_query(chunk):
        query_to_mate(chunk, 0).start()
        loop(1, 4, lambda step: query_to_z(chunk, step).start())

    loop(0, CHUNKS, send_query)

    def forward_query(chunk):
        def one(step):
            query_from_z(chunk, step).wait_recv()
            query_to_mate(chunk, step).start()

        loop(1, 4, one)

    def receive_query(chunk):
        loop(0, 4, lambda step: query_from_mate(chunk, step).wait_recv())

    base = ctx * (SPAN * HEAD) + head * SPAN
    position = base + lanes((1, SPAN))

    def attend_row(row):
        key_copy(row).wait()
        block = keys[row]
        score = jnp.dot(query[row], block, preferred_element_type=F32)
        score = jnp.where(position < lengths_ref[row], score, -1e30)
        peak = jnp.max(score, axis=1, keepdims=True)
        weight = jnp.exp2((score - peak) * SCALE)
        total = jnp.sum(weight, axis=1, keepdims=True)
        summed = lax.dot_general(
            weight.astype(BF16),
            block[:LAT],
            (((1,), (1,)), ((), ())),
            preferred_element_type=F32,
        )
        return summed * (1.0 / total), peak * SCALE + jnp.log2(total)

    def first_copy(chunk):
        return remote(
            s1.at[chunk, 1 - core], r1.at[chunk], s1_sem.at[chunk], r1_sem.at[chunk], {"head": mate}
        )

    def attend(chunk):
        results = [attend_row(chunk * CHUNK + row) for row in range(CHUNK)]
        level = put_levels([result[1] for result in results], HEADS)
        for group in range(HEAD):
            rows = slice(group * GROUP, (group + 1) * GROUP)
            for row in range(CHUNK):
                for tile in range(4):
                    s1[chunk, group % 2, group // 2, row * 4 + tile] = results[row][0][
                        rows, tile * 128 : (tile + 1) * 128
                    ].astype(BF16)
            s1[chunk, group % 2, group // 2, CHUNK * 4] = level[rows].astype(BF16)
        first_copy(chunk).start()

    def merge(blocks):
        tiles = [block[CHUNK * 4].astype(F32) for block in blocks]
        merged, levels = [], []
        for row in range(CHUNK):
            parts, level = weights_of([get_level(tile, row) for tile in tiles])
            levels.append(level)
            merged.append(
                [
                    functools.reduce(
                        jnp.add,
                        [
                            block[row * 4 + tile].astype(F32) * part
                            for block, part in zip(blocks, parts)
                        ],
                    )
                    for tile in range(4)
                ]
            )
        return merged, levels

    def second_copy(chunk, step):
        z = other_z(step)
        return remote(
            s2.at[chunk, z],
            r2.at[chunk, level_z],
            s2_sem.at[chunk, step],
            r2_sem.at[chunk, level_z],
            {"head": z * 2 + core},
        )

    def second_arrival(chunk, step):
        z = other_z(step)
        return remote(
            s2.at[chunk, z],
            r2.at[chunk, z],
            s2_sem.at[chunk, step],
            r2_sem.at[chunk, z],
            {"head": z * 2 + core},
        )

    def merge_cores(chunk):
        first_copy(chunk).wait_recv()

        def one(step):
            z = other_z(step)
            merged, levels = merge([s1.at[chunk, core, z], r1.at[chunk, z]])
            for row in range(CHUNK):
                for tile in range(4):
                    s2[chunk, z, row * 4 + tile] = merged[row][tile].astype(BF16)
            s2[chunk, z, CHUNK * 4] = put_levels(levels, GROUP).astype(BF16)

        def send(step):
            one(step)
            second_copy(chunk, step).start()

        loop(1, 4, send)
        one(0)

    def merge_z(chunk):
        loop(1, 4, lambda step: second_arrival(chunk, step).wait_recv())
        sources = [s2.at[chunk, level_z]] + [r2.at[chunk, other_z(step)] for step in (1, 2, 3)]
        merged, levels = merge(sources)
        for row in range(CHUNK):
            rows = pl.ds(pl.multiple_of((chunk * CHUNK + row) * GROUP, GROUP), GROUP)
            for tile in range(4):
                whole[tile, rows, :] = merged[row][tile]
            whole_level[rows, :] = jnp.broadcast_to(levels[row], (GROUP, 128))

    def stage(index):
        @pl.when(index < CHUNKS)
        def _():
            forward_query(index)

        @pl.when((index >= 1) & (index <= CHUNKS))
        def _():
            receive_query(index - 1)
            attend(index - 1)

        @pl.when((index >= 2) & (index <= CHUNKS + 1))
        def _():
            merge_cores(index - 2)

        @pl.when(index >= 3)
        def _():
            merge_z(index - 3)

    loop(0, CHUNKS + 3, stage)

    def to_ctx(src, dst, send_sem, recv_sem, step):
        peer = other_ctx(step)
        return remote(src(peer), dst.at[ctx], send_sem.at[peer], recv_sem.at[ctx], {"ctx": peer})

    def from_ctx(src, dst, send_sem, recv_sem, step):
        peer = other_ctx(step)
        return remote(src(peer), dst.at[peer], send_sem.at[peer], recv_sem.at[peer], {"ctx": peer})

    def to_head(src, dst, send_sem, recv_sem, step):
        peer = other_head(step)
        return remote(src(peer), dst.at[head], send_sem.at[peer], recv_sem.at[head], {"head": peer})

    def from_head(src, dst, send_sem, recv_sem, step):
        peer = other_head(step)
        return remote(src(peer), dst.at[peer], send_sem.at[peer], recv_sem.at[peer], {"head": peer})

    for member in range(GROUP):
        rows = pl.ds(member, ROWS, stride=GROUP)
        first, second = pack(jnp.concatenate([whole[tile, rows, :] for tile in range(4)], axis=1))
        s3[member, 0] = first
        s3[member, 1] = second
        level = put_levels([whole_level[rows, :]], ROWS)
        s3[member, 2] = jnp.concatenate([level, jnp.zeros_like(level)], axis=0).astype(BF16)
    exchange3 = (lambda peer: s3.at[peer], r3, s3_sem, r3_sem)
    loop(1, CTX, lambda step: to_ctx(*exchange3, step).start())
    r3[ctx] = s3[ctx]
    value_copy.wait()
    loop(1, CTX, lambda step: from_ctx(*exchange3, step).wait_recv())
    parts, _ = weights_of([get_level(r3[peer, 2].astype(F32)[0:8], 0) for peer in range(CTX)])
    latent_out = functools.reduce(
        jnp.add, [unpack(r3[peer, 0], r3[peer, 1]) * parts[peer] for peer in range(CTX)]
    )
    head_out = jnp.dot(latent_out.astype(BF16), value_up[...], preferred_element_type=F32)
    s4[...] = head_out.astype(BF16).astype(F32)
    exchange4 = (lambda peer: s4, r4, s4_sem, r4_sem)
    loop(1, CTX, lambda step: to_ctx(*exchange4, step).start())
    r4[ctx] = s4[...]
    output_copy.wait()
    loop(1, CTX, lambda step: from_ctx(*exchange4, step).wait_recv())
    gathered = jnp.concatenate([r4[peer] for peer in range(CTX)], axis=1).astype(BF16)
    partial = lax.dot_general(
        gathered, w_out[...], (((1,), (1,)), ((), ())), preferred_element_type=F32
    )
    first, second = pack(partial)
    s5[0] = first
    s5[1] = second
    exchange5 = (lambda peer: s5, r5, s5_sem, r5_sem)
    loop(1, HEAD, lambda step: to_head(*exchange5, step).start())
    r5[head] = s5[...]
    loop(1, HEAD, lambda step: from_head(*exchange5, step).wait_recv())
    attn = functools.reduce(jnp.add, [unpack(r5[peer, 0], r5[peer, 1]) for peer in range(HEAD)])
    first, second = pack(attn)
    s6[0] = first
    s6[1] = second
    exchange6 = (lambda peer: s6, r6, s6_sem, r6_sem)
    loop(1, CTX, lambda step: to_ctx(*exchange6, step).start())
    r6[ctx] = s6[...]
    attn_ref[...] = attn[:, 0:COLS].astype(BF16)
    gate_copy.wait()
    up_copy.wait()
    loop(1, CTX, lambda step: from_ctx(*exchange6, step).wait_recv())
    squares = jnp.zeros((ROWS, 512), F32)
    gate = jnp.zeros((ROWS, 256), F32)
    upper = jnp.zeros((ROWS, 256), F32)
    for peer in range(CTX):
        features = unpack(r6[peer, 0], r6[peer, 1])
        squares += features * features
        features = features[:, 0:COLS].astype(BF16)
        rows = pl.ds(peer * COLS, COLS)
        gate += jnp.dot(features, w_gate[rows, :], preferred_element_type=F32)
        upper += jnp.dot(features, w_up[rows, :], preferred_element_type=F32)
    mean = jnp.sum(squares, axis=1, keepdims=True) * (1.0 / D)
    factor = 1.0 / jnp.sqrt(mean + 1e-06)
    gate = gate * factor
    upper = upper * factor
    hidden = (gate / (1.0 + jnp.exp(-gate)) * upper).astype(BF16)
    chosen = jnp.where(ids_ref[...] == ctx, gates_ref[...], 0.0)
    select = jnp.sum(chosen, axis=1, keepdims=True)
    down_copy.wait()
    result = jnp.dot(hidden, w_down[...], preferred_element_type=F32) * select
    for peer in range(CTX):
        left = peer * COLS // 128 * 128
        first, second = pack(result[:, left : left + 512])
        s7[peer, 0] = first
        s7[peer, 1] = second
    exchange7 = (lambda peer: s7.at[peer], r7, s7_sem, r7_sem)
    loop(1, CTX, lambda step: to_ctx(*exchange7, step).start())
    r7[ctx] = s7[ctx]
    loop(1, CTX, lambda step: from_ctx(*exchange7, step).wait_recv())
    share = functools.reduce(jnp.add, [unpack(r7[peer, 0], r7[peer, 1]) for peer in range(CTX)])
    share = jnp.where(lax.rem(ctx, 2) == 1, pltpu.roll(share, 512 - COLS % 128, 1), share)
    for peer in range(HEAD):
        moved = share if peer == 0 else pltpu.roll(share, 512 - peer * OUT, 1)
        s8[peer] = moved[:, 0:128]
    exchange8 = (lambda peer: s8.at[peer], r8, s8_sem, r8_sem)
    loop(1, HEAD, lambda step: to_head(*exchange8, step).start())
    r8[head] = s8[head]
    loop(1, HEAD, lambda step: from_head(*exchange8, step).wait_recv())
    final = functools.reduce(jnp.add, [r8[peer] for peer in range(HEAD)])
    expert_ref[...] = final[:, 0:OUT].astype(BF16)

    def drain(chunk):
        def queries(step):
            query_to_z(chunk, step).wait_send()
            query_to_mate(chunk, step).wait_send()
            second_copy(chunk, step).wait_send()

        loop(1, 4, queries)
        query_to_mate(chunk, 0).wait_send()
        first_copy(chunk).wait_send()

    loop(0, CHUNKS, drain)

    def drain_ctx(step):
        for exchange in (exchange3, exchange4, exchange6, exchange7):
            to_ctx(*exchange, step).wait_send()

    def drain_head(step):
        for exchange in (exchange5, exchange8):
            to_head(*exchange, step).wait_send()

    loop(1, CTX, drain_ctx)
    loop(1, HEAD, drain_head)


def body(
    q_nope,
    q_rope,
    latent_cache,
    lengths,
    w_key_absorb,
    w_value_up,
    w_output,
    w_gate,
    w_up,
    w_down,
    expert_ids,
    gate_weights,
):
    vmem = pl.BlockSpec(memory_space=pltpu.VMEM)
    hbm = pl.BlockSpec(memory_space=pl.ANY)
    dma = pltpu.SemaphoreType.DMA
    return pl.pallas_call(
        kernel,
        out_shape=(
            jax.ShapeDtypeStruct((ROWS, COLS), BF16),
            jax.ShapeDtypeStruct((ROWS, OUT), BF16),
        ),
        in_specs=[pl.BlockSpec(memory_space=pltpu.SMEM)] + [vmem] * 4 + [hbm] * 7,
        out_specs=(vmem, vmem),
        scratch_shapes=[
            pltpu.VMEM((ROWS, KEY, SPAN), BF16),
            pltpu.VMEM((GROUP, NOPE, LAT), BF16),
            pltpu.VMEM((LAT, NOPE), BF16),
            pltpu.VMEM((512, GROUP * NOPE), BF16),
            pltpu.VMEM((D, 256), BF16),
            pltpu.VMEM((D, 256), BF16),
            pltpu.VMEM((256, D), BF16),
            pltpu.VMEM((ROWS, HEADS, KEY), BF16),
            pltpu.VMEM((CHUNKS, 2, 4, TILES, 16, 128), BF16),
            pltpu.VMEM((CHUNKS, 4, TILES, 16, 128), BF16),
            pltpu.VMEM((CHUNKS, 4, TILES, 16, 128), BF16),
            pltpu.VMEM((CHUNKS, 4, TILES, 16, 128), BF16),
            pltpu.VMEM((4, ROWS * GROUP, 128), F32),
            pltpu.VMEM((ROWS * GROUP, 128), F32),
            pltpu.VMEM((CTX, 3, 16, 128), BF16),
            pltpu.VMEM((CTX, 3, 16, 128), BF16),
            pltpu.VMEM((ROWS, NOPE), F32),
            pltpu.VMEM((CTX, ROWS, NOPE), F32),
            pltpu.VMEM((2, 16, 128), BF16),
            pltpu.VMEM((HEAD, 2, 16, 128), BF16),
            pltpu.VMEM((2, 16, 128), BF16),
            pltpu.VMEM((CTX, 2, 16, 128), BF16),
            pltpu.VMEM((CTX, 2, 16, 128), BF16),
            pltpu.VMEM((CTX, 2, 16, 128), BF16),
            pltpu.VMEM((HEAD, ROWS, 128), F32),
            pltpu.VMEM((HEAD, ROWS, 128), F32),
            dma((ROWS,)),
            dma((6,)),
            dma((CHUNKS, 8)),
            dma((CHUNKS, 4)),
            dma((CHUNKS, 4)),
            dma((CHUNKS,)),
            dma((CHUNKS,)),
            dma((CHUNKS, 4)),
            dma((CHUNKS, 4)),
            dma((CTX,)),
            dma((CTX,)),
            dma((CTX,)),
            dma((CTX,)),
            dma((HEAD,)),
            dma((HEAD,)),
            dma((CTX,)),
            dma((CTX,)),
            dma((CTX,)),
            dma((CTX,)),
            dma((HEAD,)),
            dma((HEAD,)),
        ],
        compiler_params=pltpu.CompilerParams(
            collective_id=0, has_side_effects=True, vmem_limit_bytes=56 * 2**20
        ),
    )(
        lengths,
        q_nope,
        q_rope,
        expert_ids,
        gate_weights,
        jnp.swapaxes(latent_cache, 1, 2),
        w_key_absorb,
        w_value_up,
        w_output.T,
        w_gate,
        w_up,
        w_down,
    )


def solution(mesh):
    return jax.shard_map(
        body,
        mesh=mesh,
        in_specs=(
            P(None, "head", None),
            P(None, "head", None),
            P(None, "ctx", None),
            P(),
            P("head", None, None),
            P("head", None, None),
            P("head", "ctx"),
            P("ctx", None, "head"),
            P("ctx", None, "head"),
            P("ctx", "head", None),
            P(),
            P(),
        ),
        out_specs=(P(None, "ctx"), P(None, ("ctx", "head"))),
        check_vma=False,
    )
```

time: 272 us -> 69.6 us (0.26)
  blocking collectives: 152 us -> 0 us
  matrix products: 67.9 us -> 0 us
  Pallas kernels: 0 us -> 66.2 us
  other arithmetic: 20.8 us -> 0 us
  waiting for transfers between devices: 13.5 us -> 0 us
  between operations: 14.1 us -> 0.64 us
    unnamed x1 -> x0, blocking collectives: 72.1 us -> none
    dot_general x6 -> x0, matrix products: 67.9 us -> none  [the longest x1 28.7 us: attend(): jnp.einsum('bhc,btc->bht', query, cache, preferred_element_type=jnp.float32)]
    pallas_call x0 -> x1, Pallas kernels: none -> 66.2 us  [body(): pl.pallas_call(kernel, out_shape=(jax.ShapeDtypeStruct((ROWS, COLS), BF16...]
    all_gather x3 -> x0, blocking collectives: 56.5 us -> none  [the longest x2 38.2 us: merged(): gathered = jax.tree.map(lambda a: lax.all_gather(a, axis), part)]
    psum x1 -> x0, blocking collectives: 22.9 us -> none  [body(): attn_out = lax.psum(partial_proj, 'head').astype(jnp.bfloat16)]
    add x31 -> x0, other arithmetic: 16.3 us -> none  [the longest x15 16.1 us: join_partials(): summed = first[2] * left[..., None] + second[2] * right[..., None]]
    all_gather x1 -> x0, waiting for transfers between devices: 13.5 us -> none  [merged(): gathered = jax.tree.map(lambda a: lax.all_gather(a, axis), part)]
    reduce_sum x3 -> x0, other arithmetic: 3.59 us -> none  [the longest x1 3.3 us: attend(): total = jnp.sum(weight, axis=-1)]
  transfers between devices with their start and end apart: 1 -> 0, of which waited for: 1 -> 0; matrix products, arithmetic and copies ran while one was open for 1% -> 0% of each run, Pallas kernels for 0% -> 0%
where the time goes in v1:
time: 69.6 us; the launch traced here: 69.4 us
  Pallas kernels  66.2 us (95%)
  local copies, waits for them, and re-layouts  2.53 us (4%)
    pallas_call x1, Pallas kernels, body(): pl.pallas_call(kernel, out_shape=(jax.ShapeDtypeStruct((ROWS, COLS), BF16...  66.2 us
    unnamed x2, local copies, waits for them, and re-layouts  2.53 us

profile of v1, /device:TPU:1, one launch (start us, length us, event | category | flops | bytes accessed | tf_op | source)
XLA Modules:
  0.0 69.4 jit_solution(14889395787660463781)
XLA Ops:
  0.6 66.2 %shard_map.131 = (bf16[8,448]{1,0:T(8,128)(2,1)}, bf16[8,56]{1,0:T(8,128)(2,1)}) custom-call(s32[8]{0:T(128)} %lengths_ref.1, bf16[8,16,128]{2,1,0:T(8,128)(2,1)} %q_nope_ref.1, bf16[8,16,64]{2,1,0:T(8,128)(2,1)} %q_rope_ref.1, s32[8,8]{1,0:T(8,128)} %ids_ref.1, f32[8,8]{1,0:T(8,128)} %gates_ref.1, bf16[8,576,8192]{2,1,0:T(8,128)(2,1)} %bitcast.cache_hbm, ...), custom_call_target="tpu_custom_call" | custom-call | tf_op jit(solution)/shard_map/pallas_call | solution.py:541
  66.9 1.3 %copy.16 = bf16[8,448]{1,0:T(8,128)(2,1)} copy(bf16[8,448]{1,0:T(8,128)(2,1)} %get-tuple-element.4) | data formatting | bytes 14336
  68.2 1.2 %copy.17 = bf16[8,56]{1,0:T(8,128)(2,1)} copy(bf16[8,56]{1,0:T(8,128)(2,1)} %get-tuple-element.5) | data formatting | bytes 1792

commit v2 on v1

v2 whole, which is shorter than its diff:
```python
import functools
import math

import jax
import jax.numpy as jnp
from jax import lax
from jax.experimental import pallas as pl
from jax.experimental.pallas import tpu as pltpu
from jax.sharding import PartitionSpec as P

ROWS = 8
HEADS = 128
NOPE = 128
ROPE = 64
LAT = 512
KEY = LAT + ROPE
D = 7168
CTX = 16
HEAD = 8
GROUP = HEADS // HEAD
SPAN = 8192 // 2
SLOTS = 6
COLS = D // CTX
OUT = COLS // HEAD
CHUNK = 2
CHUNKS = ROWS // CHUNK
TRANSPOSED = (((1,), (1,)), ((), ()))
TILES = CHUNK * 4 + 1
SCALE = (NOPE + ROPE) ** -0.5 * math.log2(math.e)
EARLY = 6
LATE = ROWS - EARLY
MESH = pl.DeviceIdType.MESH
F32 = jnp.float32
BF16 = jnp.bfloat16


def remote(src, dst, send_sem, recv_sem, device):
    return pltpu.make_async_remote_copy(
        src_ref=src,
        dst_ref=dst,
        send_sem=send_sem,
        recv_sem=recv_sem,
        device_id=device,
        device_id_type=MESH,
    )


def hops(step):
    return sum(min(part, 4 - part) for part in step)


NEAREST = sorted(((dy, dx) for dy in range(4) for dx in range(4) if dy or dx), key=hops)
FARTHEST = NEAREST[::-1]


def loop(low, high, step):
    def run(index, carry):
        step(index)
        return carry

    lax.fori_loop(low, high, run, 0)


def pack(wide):
    wide = wide.astype(BF16).astype(F32)
    first = jnp.concatenate([wide[:, 0:128], wide[:, 128:256]], axis=0).astype(BF16)
    second = jnp.concatenate([wide[:, 256:384], wide[:, 384:512]], axis=0).astype(BF16)
    return first, second


def unpack(first, second):
    first = first.astype(F32)
    second = second.astype(F32)
    return jnp.concatenate([first[0:8], first[8:16], second[0:8], second[8:16]], axis=1)


def split_three(value):
    high = value.astype(BF16).astype(F32)
    rest = value - high
    middle = rest.astype(BF16).astype(F32)
    return high, middle, rest - middle


def lanes(shape):
    return lax.broadcasted_iota(jnp.int32, shape, len(shape) - 1)


def put_levels(levels, rows):
    lane = lanes((rows, 128))
    tile = jnp.zeros((rows, 128), F32)
    for index, level in enumerate(levels):
        for part, value in enumerate(split_three(level)):
            tile = jnp.where(lane == 3 * index + part, value, tile)
    return tile


def get_level(tile, index):
    lane = lanes(tile.shape)
    wanted = (lane >= 3 * index) & (lane < 3 * index + 3)
    return jnp.sum(jnp.where(wanted, tile, 0.0), axis=1, keepdims=True)


def weights_of(levels):
    peak = functools.reduce(jnp.maximum, levels)
    parts = [jnp.exp2(level - peak) for level in levels]
    total = functools.reduce(jnp.add, parts)
    scale = 1.0 / total
    return [part * scale for part in parts], peak + jnp.log2(total)


def kernel(
    lengths_ref,
    q_nope_ref,
    q_rope_ref,
    ids_ref,
    gates_ref,
    cache_hbm,
    absorb_hbm,
    value_hbm,
    output_hbm,
    gate_hbm,
    up_hbm,
    down_hbm,
    attn_ref,
    expert_ref,
    keys,
    absorb,
    value_up,
    w_out,
    w_gate,
    w_up,
    w_down,
    query,
    s1,
    r1,
    whole,
    whole_level,
    s3,
    r3,
    s4,
    r4,
    heads,
    s5,
    r5,
    s6,
    r6,
    s7,
    r7,
    s8,
    r8,
    key_sem,
    weight_sem,
    query_sem,
    s1_sem,
    r1_sem,
    s3_sem,
    r3_sem,
    s4_sem,
    r4_sem,
    s5_sem,
    r5_sem,
    s6_sem,
    r6_sem,
    s7_sem,
    r7_sem,
    s8_sem,
    r8_sem,
):
    ctx = lax.axis_index("ctx")
    head = lax.axis_index("head")
    core = lax.rem(head, 2)
    mate = {"head": head + 1 - 2 * core}

    def other_ctx(step):
        dy, dx = step
        return lax.rem(ctx // 4 + dy, 4) * 4 + lax.rem(lax.rem(ctx, 4) + dx, 4)

    def other_head(step):
        return lax.rem(head + step, HEAD)

    def key_copy(row):
        return pltpu.make_async_copy(
            cache_hbm.at[row, :, pl.ds(pl.multiple_of(core * SPAN, SPAN), SPAN)],
            keys.at[lax.rem(row, SLOTS)],
            key_sem.at[row],
        )

    absorb_copy = pltpu.make_async_copy(absorb_hbm, absorb, weight_sem.at[0])
    value_copy = pltpu.make_async_copy(value_hbm, value_up, weight_sem.at[1])
    output_copy = pltpu.make_async_copy(output_hbm, w_out.at[pl.ds(0, COLS)], weight_sem.at[2])
    gate_copy = pltpu.make_async_copy(gate_hbm.at[0], w_gate, weight_sem.at[3])
    up_copy = pltpu.make_async_copy(up_hbm.at[0], w_up, weight_sem.at[4])
    down_copy = pltpu.make_async_copy(down_hbm.at[0], w_down, weight_sem.at[5])
    absorb_copy.start()
    barrier = pltpu.get_barrier_semaphore()

    def greet(device):
        pl.semaphore_signal(barrier, inc=1, device_id=device, device_id_type=MESH)

    for step in FARTHEST:
        greet({"ctx": other_ctx(step)})
    loop(1, HEAD, lambda step: greet({"head": other_head(step)}))
    loop(0, SLOTS, lambda row: key_copy(row).start())
    value_copy.start()
    output_copy.start()

    w_out[pl.ds(COLS, 512 - COLS), :] = jnp.zeros((512 - COLS, GROUP * NOPE), BF16)
    flat = q_nope_ref[...].reshape(ROWS * GROUP, NOPE).astype(F32)
    which = lax.rem(lax.broadcasted_iota(jnp.int32, (ROWS * GROUP, NOPE), 0), GROUP)
    blocks = [jnp.where(which == h, flat, 0.0).astype(BF16) for h in range(GROUP)]
    wide_query = jnp.concatenate(blocks, axis=1)
    absorb_copy.wait()
    latent = jnp.dot(
        wide_query,
        absorb[...].reshape(GROUP * NOPE, LAT),
        preferred_element_type=F32,
    ).astype(BF16)
    mine = pl.ds(pl.multiple_of(core * GROUP, GROUP), GROUP)
    query[:, mine, 0:LAT] = latent.reshape(ROWS, GROUP, LAT)
    query[:, mine, LAT:KEY] = q_rope_ref[...]
    pl.semaphore_wait(barrier, HEAD - 1 + CTX - 1)
    query_copy = remote(
        query.at[:, mine], query.at[:, mine], query_sem.at[0], query_sem.at[1], mate
    )
    query_copy.start()
    query_copy.wait_recv()

    position = ctx * (2 * SPAN) + core * SPAN + lanes((1, SPAN))

    def attend_row(row):
        key_copy(row).wait()
        block = keys.at[lax.rem(row, SLOTS)]
        score = jnp.dot(query[row], block[...], preferred_element_type=F32)
        score = jnp.where(position < lengths_ref[row], score, -1e30)
        peak = jnp.max(score, axis=1, keepdims=True)
        weight = jnp.exp2((score - peak) * SCALE)
        total = jnp.sum(weight, axis=1, keepdims=True)
        summed = lax.dot_general(
            block[0:LAT], weight.astype(BF16), TRANSPOSED, preferred_element_type=F32
        )
        return summed.T * (1.0 / total), peak * SCALE + jnp.log2(total)

    def first_copy(chunk):
        return remote(
            s1.at[chunk, 1 - core], r1.at[chunk], s1_sem.at[chunk], r1_sem.at[chunk], mate
        )

    def attend(chunk):
        results = [attend_row(chunk * CHUNK + row) for row in range(CHUNK)]
        level = put_levels([result[1] for result in results], 2 * GROUP)
        for group in range(2):
            rows = slice(group * GROUP, (group + 1) * GROUP)
            for row in range(CHUNK):
                for tile in range(4):
                    s1[chunk, group, row * 4 + tile] = results[row][0][
                        rows, tile * 128 : (tile + 1) * 128
                    ].astype(BF16)
            s1[chunk, group, CHUNK * 4] = level[rows].astype(BF16)
        first_copy(chunk).start()

    def merge_cores(chunk):
        first_copy(chunk).wait_recv()
        blocks = [s1.at[chunk, core], r1.at[chunk]]
        tiles = [block[CHUNK * 4].astype(F32) for block in blocks]
        for row in range(CHUNK):
            parts, level = weights_of([get_level(tile, row) for tile in tiles])
            rows = pl.ds(pl.multiple_of((chunk * CHUNK + row) * GROUP, GROUP), GROUP)
            for tile in range(4):
                whole[rows, tile * 128 : (tile + 1) * 128] = functools.reduce(
                    jnp.add,
                    [
                        block[row * 4 + tile].astype(F32) * part
                        for block, part in zip(blocks, parts)
                    ],
                )
            whole_level[rows, :] = jnp.broadcast_to(level, (GROUP, 128))

    def to_ctx(src, dst, send_sem, recv_sem, step):
        peer = other_ctx(step)
        return remote(src(peer), dst.at[ctx], send_sem.at[peer], recv_sem.at[ctx], {"ctx": peer})

    def from_ctx(src, dst, send_sem, recv_sem, step):
        peer = other_ctx(step)
        return remote(src(peer), dst.at[peer], send_sem.at[peer], recv_sem.at[peer], {"ctx": peer})

    def to_head(src, dst, send_sem, recv_sem, step):
        peer = other_head(step)
        return remote(src(peer), dst.at[head], send_sem.at[peer], recv_sem.at[head], {"head": peer})

    def from_head(src, dst, send_sem, recv_sem, step):
        peer = other_head(step)
        return remote(src(peer), dst.at[peer], send_sem.at[peer], recv_sem.at[peer], {"head": peer})

    exchange3 = (lambda peer: s3, r3, s3_sem, r3_sem)
    exchange4 = (lambda peer: s4, r4, s4_sem, r4_sem)
    exchange5 = (lambda peer: s5, r5, s5_sem, r5_sem)
    exchange6 = (lambda peer: s6, r6, s6_sem, r6_sem)
    exchange7 = (lambda peer: s7.at[peer], r7, s7_sem, r7_sem)
    exchange8 = (lambda peer: s8.at[peer], r8, s8_sem, r8_sem)

    def send_ctx(exchange):
        for step in FARTHEST:
            to_ctx(*exchange, step).start()

    def receive_ctx(exchange):
        for step in NEAREST:
            from_ctx(*exchange, step).wait_recv()

    def project(first, count, exchange):
        rows = pl.ds(first * GROUP, count * GROUP)
        merged = whole[rows, :]
        which = lax.rem(lax.broadcasted_iota(jnp.int32, (count * GROUP, LAT), 0), GROUP)
        blocks = [jnp.where(which == h, merged, 0.0).astype(BF16) for h in range(GROUP)]
        share = jnp.dot(
            jnp.concatenate(blocks, axis=1),
            value_up[...].reshape(GROUP * LAT, NOPE),
            preferred_element_type=F32,
        ).astype(BF16)
        src = exchange[0](0)
        src[0:count] = share.reshape(count, GROUP, NOPE)
        levels = [whole_level[pl.ds((first + row) * GROUP, GROUP), :] for row in range(count)]
        src[count] = put_levels(levels, GROUP).astype(BF16)
        send_ctx(exchange)
        exchange[1][ctx] = src[...]

    def merge_ctx(first, count, exchange):
        receive_ctx(exchange)
        arrived = exchange[1]
        tiles = [arrived[peer, count].astype(F32) for peer in range(CTX)]
        for row in range(count):
            parts, _ = weights_of([get_level(tile, row) for tile in tiles])
            heads[pl.ds((first + row) * GROUP, GROUP), :] = functools.reduce(
                jnp.add, [arrived[peer, row].astype(F32) * parts[peer] for peer in range(CTX)]
            )

    def stage(chunk):
        attend(chunk)

        @pl.when(chunk == 0)
        def _():
            loop(SLOTS, ROWS, lambda row: key_copy(row).start())
            gate_copy.start()
            up_copy.start()
            down_copy.start()

        @pl.when(chunk >= 1)
        def _():
            merge_cores(chunk - 1)

    loop(0, CHUNKS - 1, stage)
    merge_cores(CHUNKS - 2)
    value_copy.wait()
    project(0, EARLY, exchange3)
    attend(CHUNKS - 1)
    merge_cores(CHUNKS - 1)
    project(EARLY, LATE, exchange4)
    merge_ctx(0, EARLY, exchange3)
    output_copy.wait()
    merge_ctx(EARLY, LATE, exchange4)
    gathered = [heads[pl.ds(member, ROWS, stride=GROUP), :] for member in range(GROUP)]
    partial = lax.dot_general(
        jnp.concatenate(gathered, axis=1).astype(BF16),
        w_out[...],
        TRANSPOSED,
        preferred_element_type=F32,
    )
    s5[0], s5[1] = pack(partial)
    loop(1, HEAD, lambda step: to_head(*exchange5, step).start())
    r5[head] = s5[...]
    loop(1, HEAD, lambda step: from_head(*exchange5, step).wait_recv())
    attn = functools.reduce(jnp.add, [unpack(r5[peer, 0], r5[peer, 1]) for peer in range(HEAD)])
    s6[0], s6[1] = pack(attn)
    send_ctx(exchange6)
    r6[ctx] = s6[...]
    attn_ref[...] = attn
    gate_copy.wait()
    up_copy.wait()
    squares = jnp.zeros((ROWS, 512), F32)
    gate = jnp.zeros((ROWS, 256), F32)
    upper = jnp.zeros((ROWS, 256), F32)
    for step in [(0, 0)] + NEAREST:
        peer = other_ctx(step)
        if step != (0, 0):
            from_ctx(*exchange6, step).wait_recv()
        features = unpack(r6[peer, 0], r6[peer, 1])
        squares += features * features
        features = features[:, 0:COLS].astype(BF16)
        rows = pl.ds(pl.multiple_of(peer * COLS, COLS), COLS)
        gate += jnp.dot(features, w_gate[rows, :], preferred_element_type=F32)
        upper += jnp.dot(features, w_up[rows, :], preferred_element_type=F32)
    mean = jnp.sum(squares, axis=1, keepdims=True) * (1.0 / D)
    factor = 1.0 / jnp.sqrt(mean + 1e-06)
    gate = gate * factor
    upper = upper * factor
    hidden = (gate / (1.0 + jnp.exp(-gate)) * upper).astype(BF16)
    chosen = jnp.where(ids_ref[...] == ctx, gates_ref[...], 0.0)
    select = jnp.sum(chosen, axis=1, keepdims=True)
    down_copy.wait()
    result = jnp.dot(hidden, w_down[...], preferred_element_type=F32) * select
    for peer in range(CTX):
        left = peer * COLS // 128 * 128
        s7[peer, 0], s7[peer, 1] = pack(result[:, left : left + 512])
    send_ctx(exchange7)
    share = unpack(s7[ctx, 0], s7[ctx, 1])
    for step in NEAREST:
        peer = other_ctx(step)
        from_ctx(*exchange7, step).wait_recv()
        share += unpack(r7[peer, 0], r7[peer, 1])
    share = jnp.where(lax.rem(ctx, 2) == 1, pltpu.roll(share, 512 - COLS % 128, 1), share)
    for peer in range(HEAD):
        moved = share if peer == 0 else pltpu.roll(share, 512 - peer * OUT, 1)
        s8[peer] = moved[:, 0:128]
    loop(1, HEAD, lambda step: to_head(*exchange8, step).start())
    r8[head] = s8[head]
    loop(1, HEAD, lambda step: from_head(*exchange8, step).wait_recv())
    expert_ref[...] = functools.reduce(jnp.add, [r8[peer] for peer in range(HEAD)])

    query_copy.wait_send()
    loop(0, CHUNKS, lambda chunk: first_copy(chunk).wait_send())
    for exchange in (exchange3, exchange4, exchange6, exchange7):
        for step in NEAREST:
            to_ctx(*exchange, step).wait_send()

    def drain_head(step):
        to_head(*exchange5, step).wait_send()
        to_head(*exchange8, step).wait_send()

    loop(1, HEAD, drain_head)


def finish(attn_ref, expert_ref, attn_out_ref, expert_out_ref):
    attn_out_ref[...] = attn_ref[:, 0:COLS].astype(BF16)
    expert_out_ref[...] = expert_ref[:, 0:OUT].astype(BF16)


def body(
    q_nope,
    q_rope,
    latent_cache,
    lengths,
    w_key_absorb,
    w_value_up,
    w_output,
    w_gate,
    w_up,
    w_down,
    expert_ids,
    gate_weights,
):
    vmem = pl.BlockSpec(memory_space=pltpu.VMEM)
    hbm = pl.BlockSpec(memory_space=pl.ANY)
    dma = pltpu.SemaphoreType.DMA
    attn, expert = pl.pallas_call(
        kernel,
        out_shape=(
            jax.ShapeDtypeStruct((ROWS, 512), F32),
            jax.ShapeDtypeStruct((ROWS, 128), F32),
        ),
        in_specs=[pl.BlockSpec(memory_space=pltpu.SMEM)] + [vmem] * 4 + [hbm] * 7,
        out_specs=(vmem, vmem),
        scratch_shapes=[
            pltpu.VMEM((SLOTS, KEY, SPAN), BF16),
            pltpu.VMEM((GROUP, NOPE, LAT), BF16),
            pltpu.VMEM((GROUP, LAT, NOPE), BF16),
            pltpu.VMEM((512, GROUP * NOPE), BF16),
            pltpu.VMEM((D, 256), BF16),
            pltpu.VMEM((D, 256), BF16),
            pltpu.VMEM((256, D), BF16),
            pltpu.VMEM((ROWS, 2 * GROUP, KEY), BF16),
            pltpu.VMEM((CHUNKS, 2, TILES, 16, 128), BF16),
            pltpu.VMEM((CHUNKS, TILES, 16, 128), BF16),
            pltpu.VMEM((ROWS * GROUP, LAT), F32),
            pltpu.VMEM((ROWS * GROUP, 128), F32),
            pltpu.VMEM((EARLY + 1, 16, 128), BF16),
            pltpu.VMEM((CTX, EARLY + 1, 16, 128), BF16),
            pltpu.VMEM((LATE + 1, 16, 128), BF16),
            pltpu.VMEM((CTX, LATE + 1, 16, 128), BF16),
            pltpu.VMEM((ROWS * GROUP, NOPE), F32),
            pltpu.VMEM((2, 16, 128), BF16),
            pltpu.VMEM((HEAD, 2, 16, 128), BF16),
            pltpu.VMEM((2, 16, 128), BF16),
            pltpu.VMEM((CTX, 2, 16, 128), BF16),
            pltpu.VMEM((CTX, 2, 16, 128), BF16),
            pltpu.VMEM((CTX, 2, 16, 128), BF16),
            pltpu.VMEM((HEAD, ROWS, 128), F32),
            pltpu.VMEM((HEAD, ROWS, 128), F32),
            dma((ROWS,)),
            dma((6,)),
            dma((2,)),
            dma((CHUNKS,)),
            dma((CHUNKS,)),
            dma((CTX,)),
            dma((CTX,)),
            dma((CTX,)),
            dma((CTX,)),
            dma((HEAD,)),
            dma((HEAD,)),
            dma((CTX,)),
            dma((CTX,)),
            dma((CTX,)),
            dma((CTX,)),
            dma((HEAD,)),
            dma((HEAD,)),
        ],
        compiler_params=pltpu.CompilerParams(
            collective_id=0, has_side_effects=True, vmem_limit_bytes=60 * 2**20
        ),
    )(
        lengths,
        q_nope,
        q_rope,
        expert_ids,
        gate_weights,
        jnp.swapaxes(latent_cache, 1, 2),
        w_key_absorb,
        w_value_up,
        w_output.T,
        w_gate,
        w_up,
        w_down,
    )
    return pl.pallas_call(
        finish,
        out_shape=(
            jax.ShapeDtypeStruct((ROWS, COLS), BF16),
            jax.ShapeDtypeStruct((ROWS, OUT), BF16),
        ),
    )(attn, expert)


def solution(mesh):
    return jax.shard_map(
        body,
        mesh=mesh,
        in_specs=(
            P(None, "head", None),
            P(None, "head", None),
            P(None, "ctx", None),
            P(),
            P("head", None, None),
            P("head", None, None),
            P("head", "ctx"),
            P("ctx", None, "head"),
            P("ctx", None, "head"),
            P("ctx", "head", None),
            P(),
            P(),
        ),
        out_specs=(P(None, "ctx"), P(None, ("ctx", "head"))),
        check_vma=False,
    )
```

time: 69.6 us -> 70.5 us (1.013)
  Pallas kernels: 66.2 us -> 69.7 us
  local copies, waits for them, and re-layouts: 2.53 us -> 0 us
    pallas_call x1 -> x2, Pallas kernels: 66.2 us -> 69.7 us  [the longest x1 68.3 us: body(): pl.pallas_call(kernel, out_shape=(jax.ShapeDtypeStruct((ROWS, 512), F32),...]
    unnamed x2 -> x0, local copies, waits for them, and re-layouts: 2.53 us -> none
where the time goes in v2:
time: 70.5 us; the launch traced here: 70.3 us
  Pallas kernels  69.7 us (99%)
    pallas_call x1, Pallas kernels, body(): pl.pallas_call(kernel, out_shape=(jax.ShapeDtypeStruct((ROWS, 512), F32),...  68.3 us

profile of v2, /device:TPU:1, one launch (start us, length us, event | category | flops | bytes accessed | tf_op | source)
XLA Modules:
  0.0 70.3 jit_solution(16963551916256798714)
XLA Ops:
  0.6 68.3 %shard_map.131 = (f32[8,512]{1,0:T(8,128)}, f32[8,128]{1,0:T(8,128)}) custom-call(s32[8]{0:T(128)} %lengths_ref.1, bf16[8,16,128]{2,1,0:T(8,128)(2,1)} %q_nope_ref.1, bf16[8,16,64]{2,1,0:T(8,128)(2,1)} %q_rope_ref.1, s32[8,8]{1,0:T(8,128)} %ids_ref.1, f32[8,8]{1,0:T(8,128)} %gates_ref.1, bf16[8,576,8192]{2,1,0:T(8,128)(2,1)} %bitcast.cache_hbm, ...), custom_call_target="tpu_custom_call" | custom-call | tf_op jit(solution)/shard_map/pallas_call | solution.py:453
  69.0 1.3 %shard_map.132 = (bf16[8,448]{1,0:T(8,128)(2,1)}, bf16[8,56]{1,0:T(8,128)(2,1)}) custom-call(f32[8,512]{1,0:T(8,128)} %get-tuple-element.4.attn_ref, f32[8,128]{1,0:T(8,128)} %get-tuple-element.5.expert_ref), custom_call_target="tpu_custom_call" | custom-call | tf_op jit(solution)/shard_map/pallas_call | solution.py:522

commit v3 on v2

--- a/solution.py
+++ b/solution.py
@@ -109,11 +109,11 @@
 
 
 def kernel(
-    lengths_ref,
-    q_nope_ref,
-    q_rope_ref,
-    ids_ref,
-    gates_ref,
+    lengths_hbm,
+    q_nope_hbm,
+    q_rope_hbm,
+    ids_hbm,
+    gates_hbm,
     cache_hbm,
     absorb_hbm,
     value_hbm,
@@ -121,8 +121,12 @@
     gate_hbm,
     up_hbm,
     down_hbm,
-    attn_ref,
-    expert_ref,
+    out_ref,
+    lengths_ref,
+    q_nope_ref,
+    q_rope_ref,
+    ids_ref,
+    gates_ref,
     keys,
     absorb,
     value_up,
@@ -191,7 +195,23 @@
     gate_copy = pltpu.make_async_copy(gate_hbm.at[0], w_gate, weight_sem.at[3])
     up_copy = pltpu.make_async_copy(up_hbm.at[0], w_up, weight_sem.at[4])
     down_copy = pltpu.make_async_copy(down_hbm.at[0], w_down, weight_sem.at[5])
+    small_copies = [
+        pltpu.make_async_copy(src, dst, weight_sem.at[6 + index])
+        for index, (src, dst) in enumerate(
+            (
+                (q_nope_hbm, q_nope_ref),
+                (q_rope_hbm, q_rope_ref),
+                (lengths_hbm, lengths_ref),
+                (ids_hbm, ids_ref),
+                (gates_hbm, gates_ref),
+            )
+        )
+    ]
+    small_copies[0].start()
     absorb_copy.start()
+    for copy in small_copies[1:]:
+        copy.start()
+    loop(0, 2, lambda row: key_copy(row).start())
     barrier = pltpu.get_barrier_semaphore()
 
     def greet(device):
@@ -200,11 +220,12 @@
     for step in FARTHEST:
         greet({"ctx": other_ctx(step)})
     loop(1, HEAD, lambda step: greet({"head": other_head(step)}))
-    loop(0, SLOTS, lambda row: key_copy(row).start())
+    loop(2, SLOTS, lambda row: key_copy(row).start())
     value_copy.start()
     output_copy.start()
 
     w_out[pl.ds(COLS, 512 - COLS), :] = jnp.zeros((512 - COLS, GROUP * NOPE), BF16)
+    small_copies[0].wait()
     flat = q_nope_ref[...].reshape(ROWS * GROUP, NOPE).astype(F32)
     which = lax.rem(lax.broadcasted_iota(jnp.int32, (ROWS * GROUP, NOPE), 0), GROUP)
     blocks = [jnp.where(which == h, flat, 0.0).astype(BF16) for h in range(GROUP)]
@@ -217,6 +238,7 @@
     ).astype(BF16)
     mine = pl.ds(pl.multiple_of(core * GROUP, GROUP), GROUP)
     query[:, mine, 0:LAT] = latent.reshape(ROWS, GROUP, LAT)
+    small_copies[1].wait()
     query[:, mine, LAT:KEY] = q_rope_ref[...]
     pl.semaphore_wait(barrier, HEAD - 1 + CTX - 1)
     query_copy = remote(
@@ -225,10 +247,11 @@
     query_copy.start()
     query_copy.wait_recv()
 
+    for copy in small_copies[2:]:
+        copy.wait()
     position = ctx * (2 * SPAN) + core * SPAN + lanes((1, SPAN))
 
     def attend_row(row):
-        key_copy(row).wait()
         block = keys.at[lax.rem(row, SLOTS)]
         score = jnp.dot(query[row], block[...], preferred_element_type=F32)
         score = jnp.where(position < lengths_ref[row], score, -1e30)
@@ -246,6 +269,8 @@
         )
 
     def attend(chunk):
+        for row in range(CHUNK):
+            key_copy(chunk * CHUNK + row).wait()
         results = [attend_row(chunk * CHUNK + row) for row in range(CHUNK)]
         level = put_levels([result[1] for result in results], 2 * GROUP)
         for group in range(2):
@@ -367,12 +392,17 @@
     s5[0], s5[1] = pack(partial)
     loop(1, HEAD, lambda step: to_head(*exchange5, step).start())
     r5[head] = s5[...]
+    query_copy.wait_send()
+    loop(0, CHUNKS, lambda chunk: first_copy(chunk).wait_send())
+    for exchange in (exchange3, exchange4):
+        for step in NEAREST:
+            to_ctx(*exchange, step).wait_send()
     loop(1, HEAD, lambda step: from_head(*exchange5, step).wait_recv())
     attn = functools.reduce(jnp.add, [unpack(r5[peer, 0], r5[peer, 1]) for peer in range(HEAD)])
     s6[0], s6[1] = pack(attn)
     send_ctx(exchange6)
     r6[ctx] = s6[...]
-    attn_ref[...] = attn
+    out_ref[:, 0:512] = attn
     gate_copy.wait()
     up_copy.wait()
     squares = jnp.zeros((ROWS, 512), F32)
@@ -412,25 +442,20 @@
         s8[peer] = moved[:, 0:128]
     loop(1, HEAD, lambda step: to_head(*exchange8, step).start())
     r8[head] = s8[head]
+    for step in NEAREST:
+        to_ctx(*exchange6, step).wait_send()
+    loop(1, HEAD, lambda step: to_head(*exchange5, step).wait_send())
     loop(1, HEAD, lambda step: from_head(*exchange8, step).wait_recv())
-    expert_ref[...] = functools.reduce(jnp.add, [r8[peer] for peer in range(HEAD)])
-
-    query_copy.wait_send()
-    loop(0, CHUNKS, lambda chunk: first_copy(chunk).wait_send())
-    for exchange in (exchange3, exchange4, exchange6, exchange7):
-        for step in NEAREST:
-            to_ctx(*exchange, step).wait_send()
-
-    def drain_head(step):
-        to_head(*exchange5, step).wait_send()
-        to_head(*exchange8, step).wait_send()
-
-    loop(1, HEAD, drain_head)
-
-
-def finish(attn_ref, expert_ref, attn_out_ref, expert_out_ref):
-    attn_out_ref[...] = attn_ref[:, 0:COLS].astype(BF16)
-    expert_out_ref[...] = expert_ref[:, 0:OUT].astype(BF16)
+    out_ref[:, 512:640] = functools.reduce(jnp.add, [r8[peer] for peer in range(HEAD)])
+
+    for step in NEAREST:
+        to_ctx(*exchange7, step).wait_send()
+    loop(1, HEAD, lambda step: to_head(*exchange8, step).wait_send())
+
+
+def finish(both_ref, attn_ref, expert_ref):
+    attn_ref[...] = both_ref[:, 0:COLS].astype(BF16)
+    expert_ref[...] = both_ref[:, 512 : 512 + OUT].astype(BF16)
 
 
 def body(
@@ -450,15 +475,17 @@
     vmem = pl.BlockSpec(memory_space=pltpu.VMEM)
     hbm = pl.BlockSpec(memory_space=pl.ANY)
     dma = pltpu.SemaphoreType.DMA
-    attn, expert = pl.pallas_call(
+    both = pl.pallas_call(
         kernel,
-        out_shape=(
-            jax.ShapeDtypeStruct((ROWS, 512), F32),
-            jax.ShapeDtypeStruct((ROWS, 128), F32),
-        ),
-        in_specs=[pl.BlockSpec(memory_space=pltpu.SMEM)] + [vmem] * 4 + [hbm] * 7,
-        out_specs=(vmem, vmem),
+        out_shape=pltpu.VMEM((ROWS, 640), F32),
+        in_specs=[hbm] * 12,
+        out_specs=vmem,
         scratch_shapes=[
+            pltpu.SMEM((ROWS,), jnp.int32),
+            pltpu.VMEM((ROWS, GROUP, NOPE), BF16),
+            pltpu.VMEM((ROWS, GROUP, ROPE), BF16),
+            pltpu.VMEM((ROWS, 8), jnp.int32),
+            pltpu.VMEM((ROWS, 8), F32),
             pltpu.VMEM((SLOTS, KEY, SPAN), BF16),
             pltpu.VMEM((GROUP, NOPE, LAT), BF16),
             pltpu.VMEM((GROUP, LAT, NOPE), BF16),
@@ -485,7 +512,7 @@
             pltpu.VMEM((HEAD, ROWS, 128), F32),
             pltpu.VMEM((HEAD, ROWS, 128), F32),
             dma((ROWS,)),
-            dma((6,)),
+            dma((11,)),
             dma((2,)),
             dma((CHUNKS,)),
             dma((CHUNKS,)),
@@ -525,7 +552,7 @@
             jax.ShapeDtypeStruct((ROWS, COLS), BF16),
             jax.ShapeDtypeStruct((ROWS, OUT), BF16),
         ),
-    )(attn, expert)
+    )(both)
 
 
 def solution(mesh):

time: 70.5 us -> 60.3 us (0.86)
  Pallas kernels: 69.7 us -> 58.9 us
    pallas_call x1, Pallas kernels: 68.3 us -> 57.6 us  [body(): pl.pallas_call(kernel, out_shape=pltpu.VMEM((ROWS, 640), F32), in_specs=[...]
where the time goes in v3:
time: 60.3 us; the launch traced here: 60.2 us
  Pallas kernels  58.9 us (98%)
  between operations  0.65 us (1%)
    pallas_call x1, Pallas kernels, body(): pl.pallas_call(kernel, out_shape=pltpu.VMEM((ROWS, 640), F32), in_specs=[...  57.6 us
    pallas_call x1, Pallas kernels, body(): pl.pallas_call(finish, out_shape=(jax.ShapeDtypeStruct((ROWS, COLS), BF16...  1.33 us

profile of v3, /device:TPU:1, one launch (start us, length us, event | category | flops | bytes accessed | tf_op | source)
XLA Modules:
  0.0 60.2 jit_solution(17363373101536115874)
XLA Ops:
  0.6 57.6 %shard_map.131.both_ref = f32[8,640]{1,0:T(8,128)S(1)} custom-call(s32[8]{0:T(128)} %lengths_hbm.1, bf16[8,16,128]{2,1,0:T(8,128)(2,1)} %q_nope_hbm.1, bf16[8,16,64]{2,1,0:T(8,128)(2,1)} %q_rope_hbm.1, s32[8,8]{1,0:T(8,128)} %ids_hbm.1, f32[8,8]{1,0:T(8,128)} %gates_hbm.1, bf16[8,576,8192]{2,1,0:T(8,128)(2,1)} %bitcast.cache_hbm, ...), custom_call_target="tpu_custom_call" | custom-call | tf_op jit(solution)/shard_map/pallas_call | solution.py:478
  58.2 0.0 copy-start
  58.2 0.6 copy-done
  58.8 1.3 %shard_map.132 = (bf16[8,448]{1,0:T(8,128)(2,1)}, bf16[8,56]{1,0:T(8,128)(2,1)}) custom-call(f32[8,640]{1,0:T(8,128)} %copy-done), custom_call_target="tpu_custom_call" | custom-call | tf_op jit(solution)/shard_map/pallas_call | solution.py:549
Async XLA Ops:
  58.2 0.6 %copy-start = (f32[8,640]{1,0:T(8,128)}, f32[8,640]{1,0:T(8,128)S(1)}, u32[]{:S(2)}) copy-start(f32[8,640]{1,0:T(8,128)S(1)} %shard_map.131.both_ref) | copy-start | bytes 61444

commit v4 on v3

--- a/solution.py
+++ b/solution.py
@@ -24,7 +24,6 @@
 OUT = COLS // HEAD
 CHUNK = 2
 CHUNKS = ROWS // CHUNK
-TRANSPOSED = (((1,), (1,)), ((), ()))
 TILES = CHUNK * 4 + 1
 SCALE = (NOPE + ROPE) ** -0.5 * math.log2(math.e)
 EARLY = 6
@@ -128,6 +127,8 @@
     ids_ref,
     gates_ref,
     keys,
+    values_a,
+    values_b,
     absorb,
     value_up,
     w_out,
@@ -245,33 +246,52 @@
         query.at[:, mine], query.at[:, mine], query_sem.at[0], query_sem.at[1], mate
     )
     query_copy.start()
-    query_copy.wait_recv()
-
     for copy in small_copies[2:]:
         copy.wait()
     position = ctx * (2 * SPAN) + core * SPAN + lanes((1, SPAN))
 
-    def attend_row(row):
-        block = keys.at[lax.rem(row, SLOTS)]
-        score = jnp.dot(query[row], block[...], preferred_element_type=F32)
-        score = jnp.where(position < lengths_ref[row], score, -1e30)
+    def slot(row):
+        return keys.at[lax.rem(row, SLOTS)]
+
+    def scores(row):
+        score = jnp.dot(query[row], slot(row)[...], preferred_element_type=F32)
+        return jnp.where(position < lengths_ref[row], score, -1e30)
+
+    def soften(score):
         peak = jnp.max(score, axis=1, keepdims=True)
         weight = jnp.exp2((score - peak) * SCALE)
         total = jnp.sum(weight, axis=1, keepdims=True)
-        summed = lax.dot_general(
-            block[0:LAT], weight.astype(BF16), TRANSPOSED, preferred_element_type=F32
-        )
-        return summed.T * (1.0 / total), peak * SCALE + jnp.log2(total)
+        return weight.astype(BF16), 1.0 / total, peak * SCALE + jnp.log2(total)
+
+    def turn(row, values):
+        values[...] = slot(row)[0:LAT, :].T
+
+    key_copy(0).wait()
+    turn(0, values_a)
+    query_copy.wait_recv()
+
+    def attend_pair(first, more):
+        key_copy(first + 1).wait()
+        if more:
+            key_copy(first + 2).wait()
+        score = scores(first)
+        turn(first + 1, values_b)
+        weight, inverse, level_a = soften(score)
+        score = scores(first + 1)
+        summed_a = jnp.dot(weight, values_a[...], preferred_element_type=F32) * inverse
+        if more:
+            turn(first + 2, values_a)
+        weight, inverse, level_b = soften(score)
+        summed_b = jnp.dot(weight, values_b[...], preferred_element_type=F32) * inverse
+        return (summed_a, level_a), (summed_b, level_b)
 
     def first_copy(chunk):
         return remote(
             s1.at[chunk, 1 - core], r1.at[chunk], s1_sem.at[chunk], r1_sem.at[chunk], mate
         )
 
-    def attend(chunk):
-        for row in range(CHUNK):
-            key_copy(chunk * CHUNK + row).wait()
-        results = [attend_row(chunk * CHUNK + row) for row in range(CHUNK)]
+    def attend(chunk, more):
+        results = attend_pair(chunk * CHUNK, more)
         level = put_levels([result[1] for result in results], 2 * GROUP)
         for group in range(2):
             rows = slice(group * GROUP, (group + 1) * GROUP)
@@ -359,7 +379,7 @@
             )
 
     def stage(chunk):
-        attend(chunk)
+        attend(chunk, True)
 
         @pl.when(chunk == 0)
         def _():
@@ -376,17 +396,17 @@
     merge_cores(CHUNKS - 2)
     value_copy.wait()
     project(0, EARLY, exchange3)
-    attend(CHUNKS - 1)
+    attend(CHUNKS - 1, False)
     merge_cores(CHUNKS - 1)
     project(EARLY, LATE, exchange4)
+    output_copy.wait()
+    values_a[0 : GROUP * NOPE, :] = w_out[...].T
     merge_ctx(0, EARLY, exchange3)
-    output_copy.wait()
     merge_ctx(EARLY, LATE, exchange4)
     gathered = [heads[pl.ds(member, ROWS, stride=GROUP), :] for member in range(GROUP)]
-    partial = lax.dot_general(
+    partial = jnp.dot(
         jnp.concatenate(gathered, axis=1).astype(BF16),
-        w_out[...],
-        TRANSPOSED,
+        values_a[0 : GROUP * NOPE, :],
         preferred_element_type=F32,
     )
     s5[0], s5[1] = pack(partial)
@@ -487,6 +507,8 @@
             pltpu.VMEM((ROWS, 8), jnp.int32),
             pltpu.VMEM((ROWS, 8), F32),
             pltpu.VMEM((SLOTS, KEY, SPAN), BF16),
+            pltpu.VMEM((SPAN, LAT), BF16),
+            pltpu.VMEM((SPAN, LAT), BF16),
             pltpu.VMEM((GROUP, NOPE, LAT), BF16),
             pltpu.VMEM((GROUP, LAT, NOPE), BF16),
             pltpu.VMEM((512, GROUP * NOPE), BF16),
@@ -552,6 +574,7 @@
             jax.ShapeDtypeStruct((ROWS, COLS), BF16),
             jax.ShapeDtypeStruct((ROWS, OUT), BF16),
         ),
+        compiler_params=pltpu.CompilerParams(vmem_limit_bytes=2**20),
     )(both)
 
 

time: 60.3 us -> 55.7 us (0.924)
  Pallas kernels: 58.9 us -> 55 us
    pallas_call x1, Pallas kernels: 57.6 us -> 54.4 us  [body(): pl.pallas_call(kernel, out_shape=pltpu.VMEM((ROWS, 640), F32), in_specs=[...]
    pallas_call x1, Pallas kernels: 1.33 us -> 0.6 us  [body(): pl.pallas_call(finish, out_shape=(jax.ShapeDtypeStruct((ROWS, COLS), BF16...]
where the time goes in v4:
time: 55.7 us; the launch traced here: 55.6 us
  Pallas kernels  55 us (99%)
  between operations  0.64 us (1%)
    pallas_call x1, Pallas kernels, body(): pl.pallas_call(kernel, out_shape=pltpu.VMEM((ROWS, 640), F32), in_specs=[...  54.4 us

profile of v4, /device:TPU:1, one launch (start us, length us, event | category | flops | bytes accessed | tf_op | source)
XLA Modules:
  0.0 55.6 jit_solution(8182133518893078122)
XLA Ops:
  0.6 54.4 %shard_map.131.both_ref = f32[8,640]{1,0:T(8,128)S(1)} custom-call(s32[8]{0:T(128)} %lengths_hbm.1, bf16[8,16,128]{2,1,0:T(8,128)(2,1)} %q_nope_hbm.1, bf16[8,16,64]{2,1,0:T(8,128)(2,1)} %q_rope_hbm.1, s32[8,8]{1,0:T(8,128)} %ids_hbm.1, f32[8,8]{1,0:T(8,128)} %gates_hbm.1, bf16[8,576,8192]{2,1,0:T(8,128)(2,1)} %bitcast.cache_hbm, ...), custom_call_target="tpu_custom_call" | custom-call | tf_op jit(solution)/shard_map/pallas_call | solution.py:498
  55.0 0.6 %shard_map.132 = (bf16[8,448]{1,0:T(8,128)(2,1)}, bf16[8,56]{1,0:T(8,128)(2,1)}) custom-call(f32[8,640]{1,0:T(8,128)S(1)} %shard_map.131.both_ref), custom_call_target="tpu_custom_call" | custom-call | tf_op jit(solution)/shard_map/pallas_call | solution.py:571

commit v5 on v4

--- a/solution.py
+++ b/solution.py
@@ -18,15 +18,16 @@
 CTX = 16
 HEAD = 8
 GROUP = HEADS // HEAD
-SPAN = 8192 // 2
-SLOTS = 6
+SLICE = 8192
+SHARERS = (2, 4, 4, 2)
+FIRST = (0, 0, 2, 2)
 COLS = D // CTX
 OUT = COLS // HEAD
 CHUNK = 2
 CHUNKS = ROWS // CHUNK
 TILES = CHUNK * 4 + 1
 SCALE = (NOPE + ROPE) ** -0.5 * math.log2(math.e)
-EARLY = 6
+EARLY = 4
 LATE = ROWS - EARLY
 MESH = pl.DeviceIdType.MESH
 F32 = jnp.float32
@@ -126,7 +127,8 @@
     q_rope_ref,
     ids_ref,
     gates_ref,
-    keys,
+    keys2,
+    keys4,
     values_a,
     values_b,
     absorb,
@@ -135,9 +137,12 @@
     w_gate,
     w_up,
     w_down,
-    query,
-    s1,
-    r1,
+    query2,
+    query4,
+    s1_2,
+    r1_2,
+    s1_4,
+    r1_4,
     whole,
     whole_level,
     s3,
@@ -155,9 +160,13 @@
     r8,
     key_sem,
     weight_sem,
-    query_sem,
-    s1_sem,
-    r1_sem,
+    query2_sem,
+    query4_send,
+    query4_recv,
+    s1_2_sem,
+    r1_2_sem,
+    s1_4_sem,
+    r1_4_sem,
     s3_sem,
     r3_sem,
     s4_sem,
@@ -173,8 +182,17 @@
 ):
     ctx = lax.axis_index("ctx")
     head = lax.axis_index("head")
-    core = lax.rem(head, 2)
-    mate = {"head": head + 1 - 2 * core}
+    keys = {2: keys2, 4: keys4}
+    query = {2: query2, 4: query4}
+    shares = {
+        2: (s1_2, r1_2, s1_2_sem, r1_2_sem),
+        4: (s1_4, r1_4, s1_4_sem, r1_4_sem),
+    }
+    place = {sharers: lax.rem(head, sharers) for sharers in (2, 4)}
+
+    def partner(sharers, step):
+        member = lax.rem(place[sharers] + step, sharers)
+        return member, {"head": head - place[sharers] + member}
 
     def other_ctx(step):
         dy, dx = step
@@ -183,11 +201,16 @@
     def other_head(step):
         return lax.rem(head + step, HEAD)
 
+    def slot(row):
+        chunk = row // CHUNK
+        return keys[SHARERS[chunk]].at[FIRST[chunk] + row % CHUNK]
+
     def key_copy(row):
+        sharers = SHARERS[row // CHUNK]
+        span = SLICE // sharers
+        positions = pl.ds(pl.multiple_of(place[sharers] * span, span), span)
         return pltpu.make_async_copy(
-            cache_hbm.at[row, :, pl.ds(pl.multiple_of(core * SPAN, SPAN), SPAN)],
-            keys.at[lax.rem(row, SLOTS)],
-            key_sem.at[row],
+            cache_hbm.at[row, :, positions], slot(row), key_sem.at[row]
         )
 
     absorb_copy = pltpu.make_async_copy(absorb_hbm, absorb, weight_sem.at[0])
@@ -212,7 +235,8 @@
     absorb_copy.start()
     for copy in small_copies[1:]:
         copy.start()
-    loop(0, 2, lambda row: key_copy(row).start())
+    for row in range(2):
+        key_copy(row).start()
     barrier = pltpu.get_barrier_semaphore()
 
     def greet(device):
@@ -221,9 +245,15 @@
     for step in FARTHEST:
         greet({"ctx": other_ctx(step)})
     loop(1, HEAD, lambda step: greet({"head": other_head(step)}))
-    loop(2, SLOTS, lambda row: key_copy(row).start())
+    for row in range(2, 6):
+        key_copy(row).start()
     value_copy.start()
     output_copy.start()
+    for row in range(6, ROWS):
+        key_copy(row).start()
+    gate_copy.start()
+    up_copy.start()
+    down_copy.start()
 
     w_out[pl.ds(COLS, 512 - COLS), :] = jnp.zeros((512 - COLS, GROUP * NOPE), BF16)
     small_copies[0].wait()
@@ -237,24 +267,51 @@
         absorb[...].reshape(GROUP * NOPE, LAT),
         preferred_element_type=F32,
     ).astype(BF16)
-    mine = pl.ds(pl.multiple_of(core * GROUP, GROUP), GROUP)
-    query[:, mine, 0:LAT] = latent.reshape(ROWS, GROUP, LAT)
+    latent = latent.reshape(ROWS, GROUP, LAT)
     small_copies[1].wait()
-    query[:, mine, LAT:KEY] = q_rope_ref[...]
+
+    def mine(sharers):
+        return pl.ds(pl.multiple_of(place[sharers] * GROUP, GROUP), GROUP)
+
+    for chunk in range(CHUNKS):
+        held = query[SHARERS[chunk]]
+        here = pl.ds(FIRST[chunk], CHUNK)
+        rows = slice(chunk * CHUNK, (chunk + 1) * CHUNK)
+        held[here, mine(SHARERS[chunk]), 0:LAT] = latent[rows]
+        held[here, mine(SHARERS[chunk]), LAT:KEY] = q_rope_ref[rows]
     pl.semaphore_wait(barrier, HEAD - 1 + CTX - 1)
-    query_copy = remote(
-        query.at[:, mine], query.at[:, mine], query_sem.at[0], query_sem.at[1], mate
+    block2 = query2.at[:, mine(2)]
+    query2_copy = remote(
+        block2, block2, query2_sem.at[0], query2_sem.at[1], partner(2, 1)[1]
     )
-    query_copy.start()
+    query2_copy.start()
+
+    def query4_copy(chunk, step, arrival=False):
+        member, device = partner(4, step)
+        owner = member if arrival else place[4]
+        rows = pl.ds(FIRST[chunk], CHUNK)
+        block = query4.at[rows, pl.ds(pl.multiple_of(owner * GROUP, GROUP), GROUP)]
+        return remote(
+            block,
+            block,
+            query4_send.at[FIRST[chunk] // CHUNK, member],
+            query4_recv.at[FIRST[chunk] // CHUNK, owner],
+            device,
+        )
+
+    for chunk in (1, 2):
+        for step in (1, 2, 3):
+            query4_copy(chunk, step).start()
     for copy in small_copies[2:]:
         copy.wait()
-    position = ctx * (2 * SPAN) + core * SPAN + lanes((1, SPAN))
-
-    def slot(row):
-        return keys.at[lax.rem(row, SLOTS)]
 
     def scores(row):
-        score = jnp.dot(query[row], slot(row)[...], preferred_element_type=F32)
+        chunk = row // CHUNK
+        sharers = SHARERS[chunk]
+        span = SLICE // sharers
+        position = ctx * SLICE + place[sharers] * span + lanes((1, span))
+        heads_of_row = query[sharers][FIRST[chunk] + row % CHUNK]
+        score = jnp.dot(heads_of_row, slot(row)[...], preferred_element_type=F32)
         return jnp.where(position < lengths_ref[row], score, -1e30)
 
     def soften(score):
@@ -264,52 +321,79 @@
         return weight.astype(BF16), 1.0 / total, peak * SCALE + jnp.log2(total)
 
     def turn(row, values):
-        values[...] = slot(row)[0:LAT, :].T
+        values[0 : SLICE // SHARERS[row // CHUNK], :] = slot(row)[0:LAT, :].T
+
+    def average(weight, values, inverse):
+        held = values[0 : weight.shape[1], :]
+        return jnp.dot(weight, held, preferred_element_type=F32) * inverse
 
     key_copy(0).wait()
     turn(0, values_a)
-    query_copy.wait_recv()
-
-    def attend_pair(first, more):
+    query2_copy.wait_recv()
+
+    def attend_pair(chunk):
+        first = chunk * CHUNK
+        more = chunk + 1 < CHUNKS
         key_copy(first + 1).wait()
-        if more:
-            key_copy(first + 2).wait()
         score = scores(first)
         turn(first + 1, values_b)
         weight, inverse, level_a = soften(score)
         score = scores(first + 1)
-        summed_a = jnp.dot(weight, values_a[...], preferred_element_type=F32) * inverse
+        if more:
+            key_copy(first + 2).wait()
+        summed_a = average(weight, values_a, inverse)
         if more:
             turn(first + 2, values_a)
         weight, inverse, level_b = soften(score)
-        summed_b = jnp.dot(weight, values_b[...], preferred_element_type=F32) * inverse
+        summed_b = average(weight, values_b, inverse)
         return (summed_a, level_a), (summed_b, level_b)
 
-    def first_copy(chunk):
+    def share_copy(chunk, step, arrival=False):
+        sharers = SHARERS[chunk]
+        src, dst, send_sem, recv_sem = shares[sharers]
+        member, device = partner(sharers, step)
+        source = member if arrival else place[sharers]
+        index = FIRST[chunk] // CHUNK
         return remote(
-            s1.at[chunk, 1 - core], r1.at[chunk], s1_sem.at[chunk], r1_sem.at[chunk], mate
+            src.at[index, member],
+            dst.at[index, source],
+            send_sem.at[index, member],
+            recv_sem.at[index, source],
+            device,
         )
 
-    def attend(chunk, more):
-        results = attend_pair(chunk * CHUNK, more)
-        level = put_levels([result[1] for result in results], 2 * GROUP)
-        for group in range(2):
+    def attend(chunk):
+        sharers = SHARERS[chunk]
+        if sharers == 4:
+            for step in (1, 2, 3):
+                query4_copy(chunk, step, True).wait_recv()
+        results = attend_pair(chunk)
+        src = shares[sharers][0]
+        index = FIRST[chunk] // CHUNK
+        level = put_levels([result[1] for result in results], sharers * GROUP)
+        for group in range(sharers):
             rows = slice(group * GROUP, (group + 1) * GROUP)
             for row in range(CHUNK):
                 for tile in range(4):
-                    s1[chunk, group, row * 4 + tile] = results[row][0][
+                    src[index, group, row * 4 + tile] = results[row][0][
                         rows, tile * 128 : (tile + 1) * 128
                     ].astype(BF16)
-            s1[chunk, group, CHUNK * 4] = level[rows].astype(BF16)
-        first_copy(chunk).start()
-
-    def merge_cores(chunk):
-        first_copy(chunk).wait_recv()
-        blocks = [s1.at[chunk, core], r1.at[chunk]]
+            src[index, group, CHUNK * 4] = level[rows].astype(BF16)
+        for step in range(sharers - 1, 0, -1):
+            share_copy(chunk, step).start()
+
+    def merge_shares(chunk):
+        sharers = SHARERS[chunk]
+        src, dst = shares[sharers][0:2]
+        index = FIRST[chunk] // CHUNK
+        blocks = [src.at[index, place[sharers]]]
+        for step in range(1, sharers):
+            share_copy(chunk, step, True).wait_recv()
+            blocks.append(dst.at[index, partner(sharers, step)[0]])
         tiles = [block[CHUNK * 4].astype(F32) for block in blocks]
         for row in range(CHUNK):
             parts, level = weights_of([get_level(tile, row) for tile in tiles])
-            rows = pl.ds(pl.multiple_of((chunk * CHUNK + row) * GROUP, GROUP), GROUP)
+            rows = pl.ds((chunk * CHUNK + row) * GROUP, GROUP)
             for tile in range(4):
                 whole[rows, tile * 128 : (tile + 1) * 128] = functools.reduce(
                     jnp.add,
@@ -378,26 +462,16 @@
                 jnp.add, [arrived[peer, row].astype(F32) * parts[peer] for peer in range(CTX)]
             )
 
-    def stage(chunk):
-        attend(chunk, True)
-
-        @pl.when(chunk == 0)
-        def _():
-            loop(SLOTS, ROWS, lambda row: key_copy(row).start())
-            gate_copy.start()
-            up_copy.start()
-            down_copy.start()
-
-        @pl.when(chunk >= 1)
-        def _():
-            merge_cores(chunk - 1)
-
-    loop(0, CHUNKS - 1, stage)
-    merge_cores(CHUNKS - 2)
+    attend(0)
+    attend(1)
+    merge_shares(0)
+    attend(2)
+    merge_shares(1)
     value_copy.wait()
     project(0, EARLY, exchange3)
-    attend(CHUNKS - 1, False)
-    merge_cores(CHUNKS - 1)
+    attend(3)
+    merge_shares(2)
+    merge_shares(3)
     project(EARLY, LATE, exchange4)
     output_copy.wait()
     values_a[0 : GROUP * NOPE, :] = w_out[...].T
@@ -412,8 +486,12 @@
     s5[0], s5[1] = pack(partial)
     loop(1, HEAD, lambda step: to_head(*exchange5, step).start())
     r5[head] = s5[...]
-    query_copy.wait_send()
-    loop(0, CHUNKS, lambda chunk: first_copy(chunk).wait_send())
+    query2_copy.wait_send()
+    for chunk in range(CHUNKS):
+        for step in range(1, SHARERS[chunk]):
+            if SHARERS[chunk] == 4:
+                query4_copy(chunk, step).wait_send()
+            share_copy(chunk, step).wait_send()
     for exchange in (exchange3, exchange4):
         for step in NEAREST:
             to_ctx(*exchange, step).wait_send()
@@ -506,18 +584,22 @@
             pltpu.VMEM((ROWS, GROUP, ROPE), BF16),
             pltpu.VMEM((ROWS, 8), jnp.int32),
             pltpu.VMEM((ROWS, 8), F32),
-            pltpu.VMEM((SLOTS, KEY, SPAN), BF16),
-            pltpu.VMEM((SPAN, LAT), BF16),
-            pltpu.VMEM((SPAN, LAT), BF16),
+            pltpu.VMEM((4, KEY, SLICE // 2), BF16),
+            pltpu.VMEM((4, KEY, SLICE // 4), BF16),
+            pltpu.VMEM((SLICE // 2, LAT), BF16),
+            pltpu.VMEM((SLICE // 2, LAT), BF16),
             pltpu.VMEM((GROUP, NOPE, LAT), BF16),
             pltpu.VMEM((GROUP, LAT, NOPE), BF16),
             pltpu.VMEM((512, GROUP * NOPE), BF16),
             pltpu.VMEM((D, 256), BF16),
             pltpu.VMEM((D, 256), BF16),
             pltpu.VMEM((256, D), BF16),
-            pltpu.VMEM((ROWS, 2 * GROUP, KEY), BF16),
-            pltpu.VMEM((CHUNKS, 2, TILES, 16, 128), BF16),
-            pltpu.VMEM((CHUNKS, TILES, 16, 128), BF16),
+            pltpu.VMEM((4, 2 * GROUP, KEY), BF16),
+            pltpu.VMEM((4, 4 * GROUP, KEY), BF16),
+            pltpu.VMEM((2, 2, TILES, 16, 128), BF16),
+            pltpu.VMEM((2, 2, TILES, 16, 128), BF16),
+            pltpu.VMEM((2, 4, TILES, 16, 128), BF16),
+            pltpu.VMEM((2, 4, TILES, 16, 128), BF16),
             pltpu.VMEM((ROWS * GROUP, LAT), F32),
             pltpu.VMEM((ROWS * GROUP, 128), F32),
             pltpu.VMEM((EARLY + 1, 16, 128), BF16),
@@ -536,8 +618,12 @@
             dma((ROWS,)),
             dma((11,)),
             dma((2,)),
-            dma((CHUNKS,)),
-            dma((CHUNKS,)),
+            dma((2, 4)),
+            dma((2, 4)),
+            dma((2, 2)),
+            dma((2, 2)),
+            dma((2, 4)),
+            dma((2, 4)),
             dma((CTX,)),
             dma((CTX,)),
             dma((CTX,)),

time: 55.7 us -> 52.1 us (0.935)
  Pallas kernels: 55 us -> 51.3 us
    pallas_call x1, Pallas kernels: 54.4 us -> 50.7 us  [body(): pl.pallas_call(kernel, out_shape=pltpu.VMEM((ROWS, 640), F32), in_specs=[...]
where the time goes in v5:
time: 52.1 us; the launch traced here: 52 us
  Pallas kernels  51.3 us (98%)
  between operations  0.64 us (1%)
    pallas_call x1, Pallas kernels, body(): pl.pallas_call(kernel, out_shape=pltpu.VMEM((ROWS, 640), F32), in_specs=[...  50.7 us

profile of v5, /device:TPU:1, one launch (start us, length us, event | category | flops | bytes accessed | tf_op | source)
XLA Modules:
  0.0 52.0 jit_solution(3268937751008394463)
XLA Ops:
  0.6 50.7 %shard_map.131.both_ref = f32[8,640]{1,0:T(8,128)S(1)} custom-call(s32[8]{0:T(128)} %lengths_hbm.1, bf16[8,16,128]{2,1,0:T(8,128)(2,1)} %q_nope_hbm.1, bf16[8,16,64]{2,1,0:T(8,128)(2,1)} %q_rope_hbm.1, s32[8,8]{1,0:T(8,128)} %ids_hbm.1, f32[8,8]{1,0:T(8,128)} %gates_hbm.1, bf16[8,576,8192]{2,1,0:T(8,128)(2,1)} %bitcast.cache_hbm, ...), custom_call_target="tpu_custom_call" | custom-call | tf_op jit(solution)/shard_map/pallas_call | solution.py:576
  51.4 0.6 %shard_map.132 = (bf16[8,448]{1,0:T(8,128)(2,1)}, bf16[8,56]{1,0:T(8,128)(2,1)}) custom-call(f32[8,640]{1,0:T(8,128)S(1)} %shard_map.131.both_ref), custom_call_target="tpu_custom_call" | custom-call | tf_op jit(solution)/shard_map/pallas_call | solution.py:657

commit v6 on v5

--- a/solution.py
+++ b/solution.py
@@ -331,16 +331,21 @@
     turn(0, values_a)
     query2_copy.wait_recv()
 
-    def attend_pair(chunk):
+    def nothing():
+        pass
+
+    def attend_pair(chunk, before, between):
         first = chunk * CHUNK
         more = chunk + 1 < CHUNKS
         key_copy(first + 1).wait()
+        before()
         score = scores(first)
         turn(first + 1, values_b)
         weight, inverse, level_a = soften(score)
         score = scores(first + 1)
         if more:
             key_copy(first + 2).wait()
+        between()
         summed_a = average(weight, values_a, inverse)
         if more:
             turn(first + 2, values_a)
@@ -362,12 +367,12 @@
             device,
         )
 
-    def attend(chunk):
+    def attend(chunk, before=nothing, between=nothing):
         sharers = SHARERS[chunk]
         if sharers == 4:
             for step in (1, 2, 3):
                 query4_copy(chunk, step, True).wait_recv()
-        results = attend_pair(chunk)
+        results = attend_pair(chunk, before, between)
         src = shares[sharers][0]
         index = FIRST[chunk] // CHUNK
         level = put_levels([result[1] for result in results], sharers * GROUP)
@@ -382,13 +387,16 @@
         for step in range(sharers - 1, 0, -1):
             share_copy(chunk, step).start()
 
+    def receive_shares(chunk):
+        for step in range(1, SHARERS[chunk]):
+            share_copy(chunk, step, True).wait_recv()
+
     def merge_shares(chunk):
         sharers = SHARERS[chunk]
         src, dst = shares[sharers][0:2]
         index = FIRST[chunk] // CHUNK
         blocks = [src.at[index, place[sharers]]]
         for step in range(1, sharers):
-            share_copy(chunk, step, True).wait_recv()
             blocks.append(dst.at[index, partner(sharers, step)[0]])
         tiles = [block[CHUNK * 4].astype(F32) for block in blocks]
         for row in range(CHUNK):
@@ -462,15 +470,20 @@
                 jnp.add, [arrived[peer, row].astype(F32) * parts[peer] for peer in range(CTX)]
             )
 
+    def send_early():
+        receive_shares(1)
+        value_copy.wait()
+        merge_shares(1)
+        project(0, EARLY, exchange3)
+
     attend(0)
     attend(1)
-    merge_shares(0)
-    attend(2)
-    merge_shares(1)
-    value_copy.wait()
-    project(0, EARLY, exchange3)
-    attend(3)
+    receive_shares(0)
+    attend(2, before=lambda: merge_shares(0))
+    attend(3, between=send_early)
+    receive_shares(2)
     merge_shares(2)
+    receive_shares(3)
     merge_shares(3)
     project(EARLY, LATE, exchange4)
     output_copy.wait()

time: 52.1 us -> 52.6 us (level)
  no operation moved by 1% of the time
where the time goes in v6:
time: 52.6 us; the launch traced here: 52.5 us
  Pallas kernels  51.8 us (98%)
  between operations  0.64 us (1%)
    pallas_call x1, Pallas kernels, body(): pl.pallas_call(kernel, out_shape=pltpu.VMEM((ROWS, 640), F32), in_specs=[...  51.2 us

profile of v6, /device:TPU:1, one launch (start us, length us, event | category | flops | bytes accessed | tf_op | source)
XLA Modules:
  0.0 52.5 jit_solution(16938283625431058310)
XLA Ops:
  0.6 51.2 %shard_map.131.both_ref = f32[8,640]{1,0:T(8,128)S(1)} custom-call(s32[8]{0:T(128)} %lengths_hbm.1, bf16[8,16,128]{2,1,0:T(8,128)(2,1)} %q_nope_hbm.1, bf16[8,16,64]{2,1,0:T(8,128)(2,1)} %q_rope_hbm.1, s32[8,8]{1,0:T(8,128)} %ids_hbm.1, f32[8,8]{1,0:T(8,128)} %gates_hbm.1, bf16[8,576,8192]{2,1,0:T(8,128)(2,1)} %bitcast.cache_hbm, ...), custom_call_target="tpu_custom_call" | custom-call | tf_op jit(solution)/shard_map/pallas_call | solution.py:589
  51.9 0.6 %shard_map.132 = (bf16[8,448]{1,0:T(8,128)(2,1)}, bf16[8,56]{1,0:T(8,128)(2,1)}) custom-call(f32[8,640]{1,0:T(8,128)S(1)} %shard_map.131.both_ref), custom_call_target="tpu_custom_call" | custom-call | tf_op jit(solution)/shard_map/pallas_call | solution.py:670

commit v7 on v6

--- a/solution.py
+++ b/solution.py
@@ -51,6 +51,7 @@
 
 NEAREST = sorted(((dy, dx) for dy in range(4) for dx in range(4) if dy or dx), key=hops)
 FARTHEST = NEAREST[::-1]
+HEAD_STEPS = (4, 5, 3, 2, 6, 1, 7)
 
 
 def loop(low, high, step):
@@ -334,18 +335,17 @@
     def nothing():
         pass
 
-    def attend_pair(chunk, before, between):
+    def attend_pair(chunk, beside):
         first = chunk * CHUNK
         more = chunk + 1 < CHUNKS
         key_copy(first + 1).wait()
-        before()
+        beside()
         score = scores(first)
         turn(first + 1, values_b)
         weight, inverse, level_a = soften(score)
         score = scores(first + 1)
         if more:
             key_copy(first + 2).wait()
-        between()
         summed_a = average(weight, values_a, inverse)
         if more:
             turn(first + 2, values_a)
@@ -367,12 +367,12 @@
             device,
         )
 
-    def attend(chunk, before=nothing, between=nothing):
+    def attend(chunk, beside=nothing):
         sharers = SHARERS[chunk]
         if sharers == 4:
             for step in (1, 2, 3):
                 query4_copy(chunk, step, True).wait_recv()
-        results = attend_pair(chunk, before, between)
+        results = attend_pair(chunk, beside)
         src = shares[sharers][0]
         index = FIRST[chunk] // CHUNK
         level = put_levels([result[1] for result in results], sharers * GROUP)
@@ -470,17 +470,15 @@
                 jnp.add, [arrived[peer, row].astype(F32) * parts[peer] for peer in range(CTX)]
             )
 
-    def send_early():
-        receive_shares(1)
-        value_copy.wait()
-        merge_shares(1)
-        project(0, EARLY, exchange3)
-
     attend(0)
     attend(1)
     receive_shares(0)
-    attend(2, before=lambda: merge_shares(0))
-    attend(3, between=send_early)
+    attend(2, lambda: merge_shares(0))
+    value_copy.wait()
+    receive_shares(1)
+    merge_shares(1)
+    project(0, EARLY, exchange3)
+    attend(3)
     receive_shares(2)
     merge_shares(2)
     receive_shares(3)
@@ -497,7 +495,8 @@
         preferred_element_type=F32,
     )
     s5[0], s5[1] = pack(partial)
-    loop(1, HEAD, lambda step: to_head(*exchange5, step).start())
+    for step in HEAD_STEPS:
+        to_head(*exchange5, step).start()
     r5[head] = s5[...]
     query2_copy.wait_send()
     for chunk in range(CHUNKS):
@@ -508,7 +507,8 @@
     for exchange in (exchange3, exchange4):
         for step in NEAREST:
             to_ctx(*exchange, step).wait_send()
-    loop(1, HEAD, lambda step: from_head(*exchange5, step).wait_recv())
+    for step in HEAD_STEPS[::-1]:
+        from_head(*exchange5, step).wait_recv()
     attn = functools.reduce(jnp.add, [unpack(r5[peer, 0], r5[peer, 1]) for peer in range(HEAD)])
     s6[0], s6[1] = pack(attn)
     send_ctx(exchange6)
@@ -551,17 +551,18 @@
     for peer in range(HEAD):
         moved = share if peer == 0 else pltpu.roll(share, 512 - peer * OUT, 1)
         s8[peer] = moved[:, 0:128]
-    loop(1, HEAD, lambda step: to_head(*exchange8, step).start())
+    for step in HEAD_STEPS:
+        to_head(*exchange8, step).start()
     r8[head] = s8[head]
-    for step in NEAREST:
-        to_ctx(*exchange6, step).wait_send()
-    loop(1, HEAD, lambda step: to_head(*exchange5, step).wait_send())
-    loop(1, HEAD, lambda step: from_head(*exchange8, step).wait_recv())
+    for exchange in (exchange6, exchange7):
+        for step in NEAREST:
+            to_ctx(*exchange, step).wait_send()
+    for step in HEAD_STEPS:
+        to_head(*exchange5, step).wait_send()
+        to_head(*exchange8, step).wait_send()
+    for step in HEAD_STEPS[::-1]:
+        from_head(*exchange8, step).wait_recv()
     out_ref[:, 512:640] = functools.reduce(jnp.add, [r8[peer] for peer in range(HEAD)])
-
-    for step in NEAREST:
-        to_ctx(*exchange7, step).wait_send()
-    loop(1, HEAD, lambda step: to_head(*exchange8, step).wait_send())
 
 
 def finish(both_ref, attn_ref, expert_ref):

time: 52.6 us -> 51.7 us (0.983)
  Pallas kernels: 51.8 us -> 51 us
    pallas_call x1, Pallas kernels: 51.2 us -> 50.3 us  [body(): pl.pallas_call(kernel, out_shape=pltpu.VMEM((ROWS, 640), F32), in_specs=[...]
where the time goes in v7:
time: 51.7 us; the launch traced here: 51.6 us
  Pallas kernels  51 us (99%)
  between operations  0.64 us (1%)
    pallas_call x1, Pallas kernels, body(): pl.pallas_call(kernel, out_shape=pltpu.VMEM((ROWS, 640), F32), in_specs=[...  50.3 us

profile of v7, /device:TPU:1, one launch (start us, length us, event | category | flops | bytes accessed | tf_op | source)
XLA Modules:
  0.0 51.6 jit_solution(14873721497353156084)
XLA Ops:
  0.6 50.3 %shard_map.131.both_ref = f32[8,640]{1,0:T(8,128)S(1)} custom-call(s32[8]{0:T(128)} %lengths_hbm.1, bf16[8,16,128]{2,1,0:T(8,128)(2,1)} %q_nope_hbm.1, bf16[8,16,64]{2,1,0:T(8,128)(2,1)} %q_rope_hbm.1, s32[8,8]{1,0:T(8,128)} %ids_hbm.1, f32[8,8]{1,0:T(8,128)} %gates_hbm.1, bf16[8,576,8192]{2,1,0:T(8,128)(2,1)} %bitcast.cache_hbm, ...), custom_call_target="tpu_custom_call" | custom-call | tf_op jit(solution)/shard_map/pallas_call | solution.py:590
  51.0 0.6 %shard_map.132 = (bf16[8,448]{1,0:T(8,128)(2,1)}, bf16[8,56]{1,0:T(8,128)(2,1)}) custom-call(f32[8,640]{1,0:T(8,128)S(1)} %shard_map.131.both_ref), custom_call_target="tpu_custom_call" | custom-call | tf_op jit(solution)/shard_map/pallas_call | solution.py:671
